TPU v7x, 32 devices: a whole 2x2x4 slice. The times are simulated.
32 devices in a mesh: row: 4 (over y, x), ch: 8 (over z, core).
Axes of the slice: x: 2, y: 2, z: 4, core: 2. Of those that a mesh axis runs over, the one named last changes fastest.
Arguments:
- features: bfloat16 [4, 256, 4096], P('row', None, 'ch'), may hold values from -6 to 6
- w_in: bfloat16 [4096, 4096], P(None, 'ch'), may hold values from -0.125 to 0.125
- w_group: bfloat16 [3, 3, 64, 4096], P(None, None, None, 'ch'), may hold values from -0.25 to 0.25
- w_out: bfloat16 [4096, 4096], P(None, 'ch'), may hold values from -0.125 to 0.125
- cotangent: bfloat16 [4, 256, 4096], P('row', None, 'ch'), may hold values from -6 to 6
Outputs:
- block_out: bfloat16 [4, 256, 4096], P('row', None, 'ch')
- grad_input: bfloat16 [4, 256, 4096], P('row', None, 'ch')
- grad_w_in: bfloat16 [4096, 4096], P(None, 'ch')
- grad_w_group: bfloat16 [3, 3, 64, 4096], P(None, None, None, 'ch')
- grad_w_out: bfloat16 [4096, 4096], P(None, 'ch')
All inputs are finite; a program needn't handle non-finite values.
Results may differ from a plain program's by a relative error of at most 0.017.
Values may be sent and summed in bfloat16 or wider, within the bound.
A program may use at most 64 MiB of HBM per device.

v0:
```python
import jax
import jax.numpy as jnp
from jax import lax
from jax.sharding import PartitionSpec as P


def padded_2(cells, sides, width):
    for axis, dim in sides:
        count = lax.axis_size(axis)
        ends = count - 1
        head = lax.slice_in_dim(cells, 0, width, axis=dim)
        tail = lax.slice_in_dim(cells, cells.shape[dim] - width, cells.shape[dim], axis=dim)
        cells = jnp.concatenate(
            [
                lax.ppermute(tail, axis, [(i, (i + 1) % count) for i in range(ends)]),
                cells,
                lax.ppermute(head, axis, [((i + 1) % count, i) for i in range(ends)]),
            ],
            axis=dim,
        )
    return cells


def silu_slope(values):
    sigma = jax.nn.sigmoid(values)
    return sigma * (1.0 + values * (1.0 - sigma))


def full_channels(local):
    return lax.all_gather(local, "ch", axis=2, tiled=True)


def row_rims(local):
    padded = padded_2(local, (("row", 0),), 1)
    return jnp.pad(padded, ((0, 0), (1, 1), (0, 0)))


def group_view(local, group_width):
    return local.reshape(local.shape[0], local.shape[1], local.shape[2] // group_width, group_width)


def body(features, w_in, w_group, w_out, cotangent):
    row_count, col_count, local_ch = features.shape
    group_width = w_group.shape[2]
    local_mid = w_in.shape[1]
    pixel_count = row_count * col_count
    gathered = full_channels(features)
    flat_in = gathered.reshape(pixel_count, -1)
    pre_one = jnp.dot(flat_in, w_in, preferred_element_type=jnp.float32)
    act_one = jax.nn.silu(pre_one).astype(jnp.bfloat16).reshape(row_count, col_count, local_mid)
    padded_one = group_view(row_rims(act_one), group_width)
    filters = w_group.reshape(3, 3, group_width, local_mid // group_width, group_width)
    pre_two = jnp.zeros((row_count, col_count, local_mid // group_width, group_width), jnp.float32)
    for row_tap in range(3):
        for col_tap in range(3):
            window = padded_one[row_tap : row_tap + row_count, col_tap : col_tap + col_count]
            pre_two = pre_two + jnp.einsum(
                "rcgi,igj->rcgj",
                window,
                filters[row_tap, col_tap],
                preferred_element_type=jnp.float32,
            )
    pre_two = pre_two.reshape(pixel_count, local_mid)
    act_two = jax.nn.silu(pre_two).astype(jnp.bfloat16)
    mid_full = full_channels(act_two.reshape(row_count, col_count, local_mid)).reshape(
        pixel_count, -1
    )
    branch = jnp.dot(mid_full, w_out, preferred_element_type=jnp.float32)
    flat_local = features.reshape(pixel_count, local_ch)
    block_out = (
        (flat_local.astype(jnp.float32) + branch)
        .astype(jnp.bfloat16)
        .reshape(row_count, col_count, local_ch)
    )
    grad_flat = cotangent.reshape(pixel_count, local_ch)
    blocks = lax.axis_size("ch")
    weight_rows = lax.all_to_all(w_out, "ch", split_axis=0, concat_axis=1, tiled=True)
    grad_full = lax.all_gather(cotangent, "ch", axis=2, tiled=True).reshape(
        pixel_count, blocks, local_ch
    )
    weight_blocks = weight_rows.reshape(local_mid, blocks, local_ch)
    pieces = jnp.einsum(
        "pkc,mkc->kpm", grad_full, weight_blocks, preferred_element_type=jnp.float32
    )
    rounded = lax.optimization_barrier(pieces.astype(jnp.bfloat16))
    d_two = jnp.sum(rounded.astype(jnp.float32), axis=0)
    grad_two = (d_two * silu_slope(pre_two)).astype(jnp.bfloat16)
    padded_two = group_view(
        row_rims(grad_two.reshape(row_count, col_count, local_mid)), group_width
    )
    d_one = jnp.zeros((row_count, col_count, local_mid // group_width, group_width), jnp.float32)
    for row_tap in range(3):
        for col_tap in range(3):
            window = padded_two[
                2 - row_tap : 2 - row_tap + row_count, 2 - col_tap : 2 - col_tap + col_count
            ]
            d_one = d_one + jnp.einsum(
                "rcgj,igj->rcgi",
                window,
                filters[row_tap, col_tap],
                preferred_element_type=jnp.float32,
            )
    grad_one = (d_one.reshape(pixel_count, local_mid) * silu_slope(pre_one)).astype(jnp.bfloat16)
    grad_view = group_view(grad_two.reshape(row_count, col_count, local_mid), group_width)
    tap_rows = []
    for row_tap in range(3):
        tap_line = []
        for col_tap in range(3):
            window = padded_one[row_tap : row_tap + row_count, col_tap : col_tap + col_count]
            tap_line.append(
                jnp.einsum("rcgi,rcgj->igj", window, grad_view, preferred_element_type=jnp.float32)
            )
        tap_rows.append(jnp.stack(tap_line))
    group_grad = jnp.stack(tap_rows).reshape(3, 3, group_width, local_mid)
    in_grad = lax.dot_general(
        flat_in, grad_one, (((0,), (0,)), ((), ())), preferred_element_type=jnp.float32
    )
    out_grad = lax.dot_general(
        mid_full, grad_flat, (((0,), (0,)), ((), ())), preferred_element_type=jnp.float32
    )
    d_input = (
        lax.psum_scatter(
            lax.dot_general(
                w_in, grad_one, (((1,), (1,)), ((), ())), preferred_element_type=jnp.float32
            ).astype(jnp.bfloat16),
            "ch",
            scatter_dimension=0,
            tiled=True,
        )
        .astype(jnp.float32)
        .T
    )
    grad_input = (
        (grad_flat.astype(jnp.float32) + d_input)
        .astype(jnp.bfloat16)
        .reshape(row_count, col_count, local_ch)
    )
    summed = (
        lax.psum(in_grad.astype(jnp.bfloat16), "row").astype(jnp.float32),
        lax.psum(out_grad.astype(jnp.bfloat16), "row").astype(jnp.float32),
        lax.psum(group_grad.astype(jnp.bfloat16), "row").astype(jnp.float32),
    )
    return (
        block_out,
        grad_input,
        summed[0].astype(jnp.bfloat16),
        summed[2].astype(jnp.bfloat16),
        summed[1].astype(jnp.bfloat16),
    )


def solution(mesh):
    placed = (
        P("row", None, "ch"),
        P(None, "ch"),
        P(None, None, None, "ch"),
        P(None, "ch"),
        P("row", None, "ch"),
    )
    return jax.shard_map(
        body,
        mesh=mesh,
        in_specs=placed,
        out_specs=(
            P("row", None, "ch"),
            P("row", None, "ch"),
            P(None, "ch"),
            P(None, None, None, "ch"),
            P(None, "ch"),
        ),
        check_vma=False,
    )
```

profile of v0, /device:TPU:1, one launch (start us, length us, event | category | flops | bytes accessed | tf_op | source)
XLA Modules:
  0.0 423.0 jit_solution(13745136016858358734)
XLA Ops:
  7.2 0.7 all-gather.4.cloned.1.call-update
  7.9 6.5 %all-to-all-start = ((bf16[8,512,512]{2,1,0:T(8,128)(2,1)}), bf16[8,512,512]{2,1,0:T(8,128)(2,1)}, u32[]{:S(2)}, u32[]{:S(2)}) async-start(bf16[8,512,512]{2,1,0:T(8,128)(2,1)} %bitcast.286), calls=%async_computation | async-start | bytes 8388608 | tf_op jit(solution)/shard_map/all_to_all | solution.py:77
  14.4 0.8 copy.68
  15.4 43.1 %all-gather.4.cloned.1.call-done = bf16[1,256,4096]{2,1,0:T(8,128)(2,1)} async-done(((bf16[1,256,512]{2,1,0:T(8,128)(2,1)}), bf16[1,256,4096]{2,1,0:T(8,128)(2,1)}) %all-gather.4.cloned.1.call-update) | async-done | bytes 2097168 | tf_op jit(solution)/shard_map/all_gather | solution.py:30
  58.4 4.1 fusion.8
  62.7 1.4 collective-permute-start.1
  64.1 4.0 collective-permute-start
  68.1 0.7 copy.65
  68.9 3.6 collective-permute-done.1
  72.4 0.8 collective-permute-done
  73.3 0.3 copy.103
  73.6 0.5 pad.7.clone
  74.3 0.3 convolution_add_fusion.7
  74.6 0.3 convolution_add_fusion.6
  75.1 0.3 convolution_add_fusion.4
  75.4 0.3 convolution_add_fusion.3
  75.9 1.1 convolution_add_fusion.1
  77.0 53.5 %all-gather.8.cloned.1.call-done = bf16[1,256,4096]{1,2,0:T(8,128)(2,1)} async-done(((bf16[1,256,512]{1,2,0:T(8,128)(2,1)}), bf16[1,256,4096]{1,2,0:T(8,128)(2,1)}) %all-gather.8.cloned.1.call-update) | async-done | bytes 2097168 | tf_op jit(solution)/shard_map/all_gather | solution.py:78
  130.5 10.9 %all-to-all-done = bf16[8,512,512]{2,1,0:T(8,128)(2,1)} async-done(((bf16[8,512,512]{2,1,0:T(8,128)(2,1)}), bf16[8,512,512]{2,1,0:T(8,128)(2,1)}, u32[]{:S(2)}, u32[]{:S(2)}) %all-to-all-start) | async-done | bytes 4194336 | tf_op jit(solution)/shard_map/all_to_all | solution.py:77
  141.4 4.2 fusion.10
  145.6 0.3 convert_reduce_fusion
  145.9 1.0 copy.82
  146.9 2.3 fusion.27
  149.2 2.0 copy.67
  151.2 2.0 fusion.23
  153.3 1.3 collective-permute-start.3
  154.6 4.0 collective-permute-start.2
  158.6 3.5 collective-permute-done.3
  162.1 0.9 collective-permute-done.2
  163.0 1.0 pad_maximum_fusion.1
  164.1 1.2 copy.104
  165.2 1.6 pad.8.clone
  166.8 0.4 fusion.32
  167.2 0.4 convolution_add_fusion.15
  167.6 0.3 convolution_add_fusion.14
  167.9 0.4 convolution_add_fusion.13
  168.2 0.4 convolution_add_fusion.12
  168.6 0.3 convolution_add_fusion.11
  168.9 0.4 convolution_add_fusion.10
  169.2 0.4 convolution_add_fusion.9
  169.6 1.1 convolution_add_fusion.8
  170.7 1.2 copy.81
  172.2 4.9 %fusion.1 = bf16[4096,256]{0,1:T(8,128)(2,1)} fusion(bf16[256,512]{1,0:T(8,128)(2,1)S(1)} %multiply_convert_fusion, bf16[4096,512]{1,0:T(8,128)(2,1)} %param.6), kind=kOutput, calls=%fused_computation.4 | convolution fusion | flops 1074790400 | bytes 6553600 | tf_op jit(solution)/shard_map/dot_general | solution.py:123
  177.1 0.2 all-reduce.5.cloned.1.call-start
  177.3 0.3 convolution_convert_fusion.10
  177.7 0.3 convolution_convert_fusion.9
  178.1 0.2 convolution_convert_fusion.8
  178.4 0.3 convolution_convert_fusion.7
  178.8 0.3 convolution_convert_fusion.6
  179.2 0.2 convolution_convert_fusion.5
  179.5 0.3 convolution_convert_fusion.4
  179.9 0.2 convolution_convert_fusion.11
  180.3 0.3 convolution_convert_fusion.3
  180.7 0.9 maximum_maximum_fusion
  181.5 4.9 %fusion = bf16[4096,512]{0,1:T(8,128)(2,1)} fusion(bf16[256,512]{1,0:T(8,128)(2,1)S(1)} %multiply_convert_fusion, bf16[1,256,4096]{2,1,0:T(8,128)(2,1)} %all-gather.4.cloned.1.call-done), kind=kOutput, calls=%fused_computation.2 | convolution fusion | flops 1075838976 | bytes 6553600 | tf_op jit(solution)/shard_map/dot_general | solution.py:115
  186.5 4.9 %convolution_convert_fusion = bf16[4096,512]{1,0:T(8,128)(2,1)} fusion(bf16[1,256,4096]{2,1,0:T(8,128)(2,1)} %all-gather.6.cloned.1.call-done, bf16[1,256,512]{2,1,0:T(8,128)(2,1)S(1)} %copy-done.2), kind=kOutput, calls=%fused_computation | convolution fusion | flops 1075838976 | bytes 6553600 | tf_op jit(solution)/shard_map/dot_general | solution.py:118
  191.4 1.6 copy-done
  193.0 4.2 fusion.19
  197.2 19.3 %reduce-scatter.2.cloned.1.call-done = bf16[512,256]{0,1:T(8,128)(2,1)} async-done(((bf16[4096,256]{0,1:T(8,128)(2,1)}), bf16[512,256]{0,1:T(8,128)(2,1)}) %reduce-scatter.2.cloned.1.call-update) | async-done | bytes 262160 | tf_op jit(solution)/shard_map/reduce_scatter | solution.py:122
  216.4 1.7 fusion.31
  218.1 186.5 %all-reduce.5.cloned.1.call-done = (bf16[4096,512]{0,1:T(8,128)(2,1)}, bf16[3,3,64,512]{3,2,1,0:T(8,128)(2,1)}, bf16[4096,512]{1,0:T(8,128)(2,1)}) async-done(((bf16[4096,512]{0,1:T(8,128)(2,1)}, bf16[3,3,64,512]{3,2,1,0:T(8,128)(2,1)}, bf16[4096,512]{1,0:T(8,128)(2,1)}), (bf16[4096,512]{0,1:T(8,128)(2,1)}, bf16[3,3,64,512]{3,2,1,0:T(8,128)(2,1)}, bf16[4096,512]{1,0:T(8,128)(2,1)})) %all-reduce.5.cloned.1.call-update) | async-done | bytes 8978448 | tf_op jit(solution)/shard_map/psum | solution.py:139
  404.7 6.5 %copy.92 = bf16[4096,512]{1,0:T(8,128)(2,1)} copy(bf16[4096,512]{0,1:T(8,128)(2,1)} %get-tuple-element.20) | data formatting | bytes 8388608
  411.2 0.8 copy.108
  412.0 4.5 %copy.109 = bf16[4096,512]{1,0:T(8,128)(2,1)} copy(bf16[4096,512]{1,0:T(8,128)(2,1)} %get-tuple-element.31) | data formatting | bytes 8388608
  (41 shorter events, 2.2 us)
Async XLA Ops:
  7.2 51.3 %all-gather.4.cloned.1.call-start = ((), (), s32[]{:S(2)}) async-start(), calls=%async_computation.2 | async-start | bytes 2359296 | tf_op jit(solution)/shard_map/all_gather | solution.py:30
  7.9 6.5 %copy-start.1 = (bf16[1,256,512]{2,1,0:T(8,128)(2,1)S(1)}, bf16[1,256,512]{2,1,0:T(8,128)(2,1)}, u32[]{:S(2)}) copy-start(bf16[1,256,512]{2,1,0:T(8,128)(2,1)} %param.9) | copy-start | bytes 786436
  7.9 133.5 %all-to-all-start = ((bf16[8,512,512]{2,1,0:T(8,128)(2,1)}), bf16[8,512,512]{2,1,0:T(8,128)(2,1)}, u32[]{:S(2)}, u32[]{:S(2)}) async-start(bf16[8,512,512]{2,1,0:T(8,128)(2,1)} %bitcast.286), calls=%async_computation | async-start | bytes 8388608 | tf_op jit(solution)/shard_map/all_to_all | solution.py:77
  14.4 116.1 %all-gather.8.cloned.1.call-start = ((), (), s32[]{:S(2)}) async-start(), calls=%async_computation.4 | async-start | bytes 2359296 | tf_op jit(solution)/shard_map/all_gather | solution.py:78
  15.3 171.2 %all-gather.6.cloned.1.call-start = ((), (), s32[]{:S(2)}) async-start(), calls=%async_computation.3 | async-start | bytes 2359296 | tf_op jit(solution)/shard_map/all_gather | solution.py:30
  62.5 1.6 copy-start.3
  62.5 5.6 %copy-start.6 = (bf16[3,3,64,512]{3,2,1,0:T(8,128)(2,1)S(1)}, bf16[3,3,64,512]{3,2,1,0:T(8,128)(2,1)}, u32[]{:S(2)}) copy-start(bf16[3,3,64,512]{3,2,1,0:T(8,128)(2,1)} %param.7) | copy-start | bytes 1769476
  62.7 9.8 %collective-permute-start.1 = (bf16[1,256,512]{2,1,0:T(8,128)(2,1)S(1)}, bf16[1,256,512]{2,1,0:T(8,128)(2,1)S(1)}, u32[]{:S(2)}, u32[]{:S(2)}) collective-permute-start(bf16[1,256,512]{2,1,0:T(8,128)(2,1)S(1)} %fusion.43), channel_id=1, source_target_pairs={{8,0},{16,8},{24,16},{9,1},{17,9},{25,17},{10,2},{18,10},{26,18},{... | collective-permute-start | bytes 786440 | tf_op jit(solution)/shard_map/ppermute | solution.py:17
  64.1 9.1 %collective-permute-start = (bf16[1,256,512]{2,1,0:T(8,128)(2,1)S(1)}, bf16[1,256,512]{2,1,0:T(8,128)(2,1)S(1)}, u32[]{:S(2)}, u32[]{:S(2)}) collective-permute-start(bf16[1,256,512]{2,1,0:T(8,128)(2,1)S(1)} %fusion.43), channel_id=1, source_target_pairs={{0,8},{8,16},{16,24},{1,9},{9,17},{17,25},{2,10},{10,18},{18,26},{... | collective-permute-start | bytes 786440 | tf_op jit(solution)/shard_map/ppermute | solution.py:15
  153.2 8.9 %copy-start.5 = (bf16[1,256,512]{2,1,0:T(8,128)(2,1)}, bf16[1,256,512]{2,1,0:T(8,128)(2,1)S(1)}, u32[]{:S(2)}) copy-start(bf16[1,256,512]{2,1,0:T(8,128)(2,1)S(1)} %get-tuple-element.23) | copy-start | bytes 786436
  153.2 63.2 %reduce-scatter.2.cloned.1.call-start = ((), (), s32[]{:S(2)}) async-start(), calls=%async_computation.5 | async-start | bytes 2359296 | tf_op jit(solution)/shard_map/reduce_scatter | solution.py:122
  153.3 8.8 %collective-permute-start.3 = (bf16[1,256,512]{2,1,0:T(8,128)(2,1)S(1)}, bf16[1,256,512]{2,1,0:T(8,128)(2,1)S(1)}, u32[]{:S(2)}, u32[]{:S(2)}) collective-permute-start(bf16[1,256,512]{2,1,0:T(8,128)(2,1)S(1)} %get-tuple-element.23), channel_id=1, source_target_pairs={{8,0},{16,8},{24,16},{9,1},{17,9},{25,17},{10,2},{18,10},{26,18},{... | collective-permute-start | bytes 786440 | tf_op jit(solution)/shard_map/ppermute | solution.py:17
  154.6 8.4 %collective-permute-start.2 = (bf16[1,256,512]{2,1,0:T(8,128)(2,1)S(1)}, bf16[1,256,512]{2,1,0:T(8,128)(2,1)S(1)}, u32[]{:S(2)}, u32[]{:S(2)}) collective-permute-start(bf16[1,256,512]{2,1,0:T(8,128)(2,1)S(1)} %get-tuple-element.23), channel_id=1, source_target_pairs={{0,8},{8,16},{16,24},{1,9},{9,17},{17,25},{2,10},{10,18},{18,26},{... | collective-permute-start | bytes 786440 | tf_op jit(solution)/shard_map/ppermute | solution.py:15
  169.6 2.3 copy-start.4
  177.1 227.6 %all-reduce.5.cloned.1.call-start = ((), (), s32[]{:S(2)}) async-start(), calls=%async_computation.6 | async-start | bytes 17956864 | tf_op jit(solution)/shard_map/psum | solution.py:139
  181.5 4.9 %copy-start.2 = (bf16[1,256,512]{2,1,0:T(8,128)(2,1)S(1)}, bf16[1,256,512]{2,1,0:T(8,128)(2,1)}, u32[]{:S(2)}) copy-start(bf16[1,256,512]{2,1,0:T(8,128)(2,1)} %param.9) | copy-start | bytes 786436
  191.4 1.6 copy-start
  191.4 1.6 copy-start.8
  404.7 6.5 %copy-start.7 = (bf16[3,3,64,512]{3,2,1,0:T(8,128)(2,1)S(1)}, bf16[3,3,64,512]{3,2,1,0:T(8,128)(2,1)}, u32[]{:S(2)}) copy-start(bf16[3,3,64,512]{3,2,1,0:T(8,128)(2,1)} %get-tuple-element.30) | copy-start | bytes 1769476
Sparse Core Ops, SparseCore 0:
  9.6 48.7 all-gather.3
  60.6 69.8 all-gather.7
  153.4 28.6 all-gather.5
  184.2 32.2 reduce-scatter.1
  220.8 183.8 all-reduce.4
where the time goes:
time: 424 us; the launch traced here: 423 us
  waiting for transfers between devices  323 us (76%)
  matrix products  38.5 us (9%)
  local copies, waits for them, and re-layouts  23.6 us (6%)
  starting transfers between devices  17.6 us (4%)
  between operations  14.2 us (3%)
  other arithmetic  6.35 us (1%)
    psum x1, waiting for transfers between devices, body(): lax.psum(in_grad.astype(jnp.bfloat16), 'row').astype(jnp.float32)  187 us
    all_gather x1, waiting for transfers between devices, body(): lax.all_gather(cotangent, 'ch', axis=2, tiled=True)  53.5 us
    all_gather x2, waiting for transfers between devices, full_channels(): return lax.all_gather(local, 'ch', axis=2, tiled=True)  43.1 us
    reduce_scatter x1, waiting for transfers between devices, body(): lax.psum_scatter(lax.dot_general(w_in, grad_one, (((1,), (1,)), ((), ()))...  19.3 us
    unnamed x25, local copies, waits for them, and re-layouts  16.3 us
    all_to_all x1, waiting for transfers between devices, body(): lax.all_to_all(w_out, 'ch', split_axis=0, concat_axis=1, tiled=True)  10.9 us
  transfers between devices with their start and end apart: 10, of which 9 were waited for; matrix products, arithmetic and copies ran while one was open for 10% of the time, Pallas kernels for 0%

commit v1 on v0

--- a/solution.py
+++ b/solution.py
@@ -2,6 +2,9 @@
 import jax.numpy as jnp
 from jax import lax
 from jax.sharding import PartitionSpec as P
+
+
+GATHER_BYTES = 8 * 1024 * 1024
 
 
 def padded_2(cells, sides, width):
@@ -73,17 +76,12 @@
         .reshape(row_count, col_count, local_ch)
     )
     grad_flat = cotangent.reshape(pixel_count, local_ch)
-    blocks = lax.axis_size("ch")
-    weight_rows = lax.all_to_all(w_out, "ch", split_axis=0, concat_axis=1, tiled=True)
-    grad_full = lax.all_gather(cotangent, "ch", axis=2, tiled=True).reshape(
-        pixel_count, blocks, local_ch
+    partial = lax.dot_general(
+        w_out, grad_flat, (((1,), (1,)), ((), ())), preferred_element_type=jnp.float32
+    ).astype(jnp.bfloat16)
+    d_two = (
+        lax.psum_scatter(partial, "ch", scatter_dimension=0, tiled=True).astype(jnp.float32).T
     )
-    weight_blocks = weight_rows.reshape(local_mid, blocks, local_ch)
-    pieces = jnp.einsum(
-        "pkc,mkc->kpm", grad_full, weight_blocks, preferred_element_type=jnp.float32
-    )
-    rounded = lax.optimization_barrier(pieces.astype(jnp.bfloat16))
-    d_two = jnp.sum(rounded.astype(jnp.float32), axis=0)
     grad_two = (d_two * silu_slope(pre_two)).astype(jnp.bfloat16)
     padded_two = group_view(
         row_rims(grad_two.reshape(row_count, col_count, local_mid)), group_width
@@ -112,12 +110,22 @@
             )
         tap_rows.append(jnp.stack(tap_line))
     group_grad = jnp.stack(tap_rows).reshape(3, 3, group_width, local_mid)
+    rows = lax.axis_size("row")
+    spread = rows * flat_in.size * flat_in.dtype.itemsize <= GATHER_BYTES
+    left_in, right_in, left_out, right_out = flat_in, grad_one, mid_full, grad_flat
+    if spread:
+        left_in, right_in, left_out, right_out = (
+            lax.all_gather(v, "row", axis=0, tiled=True)
+            for v in (flat_in, grad_one, mid_full, grad_flat)
+        )
     in_grad = lax.dot_general(
-        flat_in, grad_one, (((0,), (0,)), ((), ())), preferred_element_type=jnp.float32
-    )
+        left_in, right_in, (((0,), (0,)), ((), ())), preferred_element_type=jnp.float32
+    ).astype(jnp.bfloat16)
     out_grad = lax.dot_general(
-        mid_full, grad_flat, (((0,), (0,)), ((), ())), preferred_element_type=jnp.float32
-    )
+        left_out, right_out, (((0,), (0,)), ((), ())), preferred_element_type=jnp.float32
+    ).astype(jnp.bfloat16)
+    if not spread:
+        in_grad, out_grad = lax.psum((in_grad, out_grad), "row")
     d_input = (
         lax.psum_scatter(
             lax.dot_general(
@@ -135,18 +143,8 @@
         .astype(jnp.bfloat16)
         .reshape(row_count, col_count, local_ch)
     )
-    summed = (
-        lax.psum(in_grad.astype(jnp.bfloat16), "row").astype(jnp.float32),
-        lax.psum(out_grad.astype(jnp.bfloat16), "row").astype(jnp.float32),
-        lax.psum(group_grad.astype(jnp.bfloat16), "row").astype(jnp.float32),
-    )
-    return (
-        block_out,
-        grad_input,
-        summed[0].astype(jnp.bfloat16),
-        summed[2].astype(jnp.bfloat16),
-        summed[1].astype(jnp.bfloat16),
-    )
+    group_grad = lax.psum(group_grad.astype(jnp.bfloat16), "row")
+    return block_out, grad_input, in_grad, group_grad, out_grad
 
 
 def solution(mesh):

time: 424 us -> 441 us (1.040)
  waiting for transfers between devices: 323 us -> 339 us
  matrix products: 38.5 us -> 47.7 us
  starting transfers between devices: 17.6 us -> 11.3 us
    all_gather x1 -> x4, waiting for transfers between devices: 53.5 us -> 219 us  [body(): lax.all_gather(v, 'row', axis=0, tiled=True)]
    psum x1, waiting for transfers between devices: 187 us -> 39.3 us  [body(): group_grad = lax.psum(group_grad.astype(jnp.bfloat16), 'row')]
    reduce_scatter x0 -> x1, waiting for transfers between devices: none -> 15.1 us  [body(): lax.psum_scatter(partial, 'ch', scatter_dimension=0, tiled=True)]
    dot_general x3, matrix products: 14 us -> 25.3 us  [the longest x1 10.3 us: body(): lax.dot_general(left_in, right_in, (((0,), (0,)), ((), ())), preferred_el...]
    all_to_all x1 -> x0, waiting for transfers between devices: 10.9 us -> none  [body(): lax.all_to_all(w_out, 'ch', split_axis=0, concat_axis=1, tiled=True)]
    all_gather x2, waiting for transfers between devices: 43.1 us -> 36.5 us  [full_channels(): return lax.all_gather(local, 'ch', axis=2, tiled=True)]
    all_to_all x1 -> x0, starting transfers between devices: 6.52 us -> none  [body(): lax.all_to_all(w_out, 'ch', split_axis=0, concat_axis=1, tiled=True)]
    another operation x9, local copies, waits for them, and re-layouts: 0.88 us -> 6.8 us  [body(): tap_rows.append(jnp.stack(tap_line))]
  transfers between devices with their start and end apart: 10 -> 13, of which waited for: 9 -> 13; matrix products, arithmetic and copies ran while one was open for 10% -> 17% of each run, Pallas kernels for 0% -> 0%
where the time goes in v1:
time: 441 us; the launch traced here: 440 us
  waiting for transfers between devices  339 us (77%)
  matrix products  47.7 us (11%)
  local copies, waits for them, and re-layouts  21.8 us (5%)
  between operations  14.2 us (3%)
  starting transfers between devices  11.3 us (3%)
  other arithmetic  6.37 us (1%)
    all_gather x4, waiting for transfers between devices, body(): lax.all_gather(v, 'row', axis=0, tiled=True)  219 us
    psum x1, waiting for transfers between devices, body(): group_grad = lax.psum(group_grad.astype(jnp.bfloat16), 'row')  39.3 us
    all_gather x2, waiting for transfers between devices, full_channels(): return lax.all_gather(local, 'ch', axis=2, tiled=True)  36.5 us
    reduce_scatter x1, waiting for transfers between devices, body(): lax.psum_scatter(lax.dot_general(w_in, grad_one, (((1,), (1,)), ((), ()))...  18.4 us
    reduce_scatter x1, waiting for transfers between devices, body(): lax.psum_scatter(partial, 'ch', scatter_dimension=0, tiled=True)  15.1 us
    unnamed x19, local copies, waits for them, and re-layouts  10.5 us
    dot_general x1, matrix products, body(): lax.dot_general(left_in, right_in, (((0,), (0,)), ((), ())), preferred_el...  10.3 us
    dot_general x1, matrix products, body(): lax.dot_general(left_out, right_out, (((0,), (0,)), ((), ())), preferred_...  10.1 us
  transfers between devices with their start and end apart: 13, of which 13 were waited for; matrix products, arithmetic and copies ran while one was open for 17% of the time, Pallas kernels for 0%

profile of v1, /device:TPU:1, one launch (start us, length us, event | category | flops | bytes accessed | tf_op | source)
XLA Modules:
  0.0 439.9 jit_solution(13141432431532114112)
XLA Ops:
  7.2 0.7 all-gather.10.cloned.1.call-update
  7.9 4.8 %convolution_convert_fusion.1 = bf16[4096,256]{0,1:T(8,128)(2,1)} fusion(bf16[4096,512]{1,0:T(8,128)(2,1)} %param.8, bf16[1,256,512]{2,1,0:T(8,128)(2,1)} %param.9), kind=kOutput, calls=%fused_computation.8 | convolution fusion | flops 1074790400 | bytes 6553600 | tf_op jit(solution)/shard_map/dot_general | solution.py:79
  12.8 28.4 %all-gather.10.cloned.1.call-done = bf16[1,256,4096]{2,1,0:T(8,128)(2,1)} async-done(((bf16[1,256,512]{2,1,0:T(8,128)(2,1)}), bf16[1,256,4096]{2,1,0:T(8,128)(2,1)}) %all-gather.10.cloned.1.call-update) | async-done | bytes 2097168 | tf_op jit(solution)/shard_map/all_gather | solution.py:33
  41.2 4.1 fusion.16
  45.5 1.4 collective-permute-start.1
  46.9 4.0 collective-permute-start
  50.9 0.7 copy.61
  51.7 3.6 collective-permute-done.1
  55.2 0.8 collective-permute-done
  56.3 0.5 pad.7.clone
  57.0 0.3 convolution_add_fusion.7
  57.3 0.3 convolution_add_fusion.6
  57.9 0.3 convolution_add_fusion.4
  58.1 0.3 convolution_add_fusion.3
  58.7 0.3 convolution_add_fusion.1
  58.9 0.3 convolution_add_fusion
  59.2 0.8 fusion.33
  60.2 1.0 copy.63
  61.2 15.1 %reduce-scatter.3.cloned.1.call-done = bf16[512,256]{0,1:T(8,128)(2,1)} async-done(((bf16[4096,256]{0,1:T(8,128)(2,1)}), bf16[512,256]{0,1:T(8,128)(2,1)}) %reduce-scatter.3.cloned.1.call-update) | async-done | bytes 262160 | tf_op jit(solution)/shard_map/reduce_scatter | solution.py:83
  76.3 1.3 fusion.29
  77.6 1.3 collective-permute-start.3
  78.9 4.0 collective-permute-start.2
  82.9 1.8 collective-permute-done.3
  84.7 1.5 collective-permute-done.2
  86.3 1.2 copy.98
  87.5 1.6 pad.8.clone
  89.1 0.4 fusion.35
  89.5 0.4 convolution_add_fusion.15
  90.1 0.4 convolution_add_fusion.13
  90.5 0.4 convolution_add_fusion.12
  91.1 0.4 convolution_add_fusion.10
  91.5 0.4 convolution_add_fusion.9
  91.9 1.1 convolution_add_fusion.8
  92.9 1.2 copy.75
  94.4 4.9 %fusion.13 = bf16[4096,256]{0,1:T(8,128)(2,1)} fusion(bf16[256,512]{1,0:T(8,128)(2,1)S(1)} %multiply_convert_fusion, bf16[4096,512]{1,0:T(8,128)(2,1)} %param.6), kind=kOutput, calls=%fused_computation.9 | convolution fusion | flops 1074790400 | bytes 6553600 | tf_op jit(solution)/shard_map/dot_general | solution.py:131
  99.4 0.5 all-gather.14.cloned.1.call-update
  100.0 0.5 all-gather.16.cloned.1.call-update
  100.6 0.7 all-gather.20.cloned.1.call-update
  101.4 8.1 %all-gather.12.cloned.1.call-done = bf16[1,256,4096]{1,2,0:T(8,128)(2,1)} async-done(((bf16[1,256,512]{1,2,0:T(8,128)(2,1)}), bf16[1,256,4096]{1,2,0:T(8,128)(2,1)}) %all-gather.12.cloned.1.call-update) | async-done | bytes 2097168 | tf_op jit(solution)/shard_map/all_gather | solution.py:33
  109.9 0.3 convolution_convert_fusion.2
  110.2 0.7 copy.85
  110.9 0.3 convolution_convert_fusion.3
  111.2 0.7 copy.84
  112.1 0.7 copy.83
  113.1 0.7 copy.82
  114.2 0.7 copy.81
  115.1 0.7 copy.80
  116.1 0.7 copy.79
  117.1 0.7 copy.78
  117.8 0.9 convolution_convert_fusion.10
  118.7 1.0 copy.77
  119.8 2.0 maximum_maximum_fusion
  121.8 4.2 fusion.24
  126.0 18.4 %reduce-scatter.5.cloned.1.call-done = bf16[512,256]{0,1:T(8,128)(2,1)} async-done(((bf16[4096,256]{0,1:T(8,128)(2,1)}), bf16[512,256]{0,1:T(8,128)(2,1)}) %reduce-scatter.5.cloned.1.call-update) | async-done | bytes 262160 | tf_op jit(solution)/shard_map/reduce_scatter | solution.py:130
  144.4 1.7 fusion.34
  146.1 28.7 %all-gather.14.cloned.1.call-done = bf16[1024,512]{1,0:T(8,128)(2,1)} async-done(((bf16[256,512]{1,0:T(8,128)(2,1)}), bf16[1024,512]{1,0:T(8,128)(2,1)}) %all-gather.14.cloned.1.call-update) | async-done | bytes 1048592 | tf_op jit(solution)/shard_map/all_gather | solution.py:118
  174.8 89.3 %all-gather.16.cloned.1.call-done = bf16[1,1024,4096]{2,1,0:T(8,128)(2,1)} async-done(((bf16[1,256,4096]{2,1,0:T(8,128)(2,1)}), bf16[1,1024,4096]{2,1,0:T(8,128)(2,1)}) %all-gather.16.cloned.1.call-update) | async-done | bytes 8388624 | tf_op jit(solution)/shard_map/all_gather | solution.py:118
  264.1 10.3 %fusion.10 = bf16[4096,512]{0,1:T(8,128)(2,1)} fusion(bf16[1024,512]{1,0:T(8,128)(2,1)} %all-gather.14.cloned.1.call-done, bf16[1,1024,4096]{2,1,0:T(8,128)(2,1)} %all-gather.16.cloned.1.call-done), kind=kOutput, calls=%fused_computation.6 | convolution fusion | flops 4297064448 | bytes 13631488 | tf_op jit(solution)/shard_map/dot_general | solution.py:121
  274.4 6.4 %copy.86 = bf16[4096,512]{1,0:T(8,128)(2,1)} copy(bf16[4096,512]{0,1:T(8,128)(2,1)} %fusion.10) | data formatting | bytes 8388608
  280.8 11.8 %all-gather.20.cloned.1.call-done = bf16[1,1024,512]{2,1,0:T(8,128)(2,1)} async-done(((bf16[1,256,512]{2,1,0:T(8,128)(2,1)}), bf16[1,1024,512]{2,1,0:T(8,128)(2,1)}) %all-gather.20.cloned.1.call-update) | async-done | bytes 1048592 | tf_op jit(solution)/shard_map/all_gather | solution.py:118
  292.6 89.3 %all-gather.18.cloned.1.call-done = bf16[1,1024,4096]{1,2,0:T(8,128)(2,1)} async-done(((bf16[1,256,4096]{1,2,0:T(8,128)(2,1)}), bf16[1,1024,4096]{1,2,0:T(8,128)(2,1)}) %all-gather.18.cloned.1.call-update) | async-done | bytes 8388624 | tf_op jit(solution)/shard_map/all_gather | solution.py:118
  381.9 10.1 %fusion.7 = bf16[4096,512]{1,0:T(8,128)(2,1)} fusion(bf16[1,1024,4096]{1,2,0:T(8,128)(2,1)} %all-gather.18.cloned.1.call-done, bf16[1,1024,512]{2,1,0:T(8,128)(2,1)} %all-gather.20.cloned.1.call-done), kind=kOutput, calls=%fused_computation.5 | convolution fusion | flops 4297064448 | bytes 13631488 | tf_op jit(solution)/shard_map/dot_general | solution.py:124
  392.1 39.3 %all-reduce.4.cloned.1.call-done = bf16[3,3,64,512]{3,2,1,0:T(8,128)(2,1)} async-done(((bf16[3,3,64,512]{3,2,1,0:T(8,128)(2,1)}), bf16[3,3,64,512]{3,2,1,0:T(8,128)(2,1)}) %all-reduce.4.cloned.1.call-update) | async-done | bytes 589840 | tf_op jit(solution)/shard_map/psum | solution.py:146
  431.4 1.9 copy.100
  (45 shorter events, 4.3 us)
Async XLA Ops:
  7.2 34.1 %all-gather.10.cloned.1.call-start = ((), (), s32[]{:S(2)}) async-start(), calls=%async_computation.2 | async-start | bytes 2359296 | tf_op jit(solution)/shard_map/all_gather | solution.py:33
  7.9 68.4 %reduce-scatter.3.cloned.1.call-start = ((), (), s32[]{:S(2)}) async-start(), calls=%async_computation.4 | async-start | bytes 2359296 | tf_op jit(solution)/shard_map/reduce_scatter | solution.py:83
  12.8 96.7 %all-gather.12.cloned.1.call-start = ((), (), s32[]{:S(2)}) async-start(), calls=%async_computation.3 | async-start | bytes 2359296 | tf_op jit(solution)/shard_map/all_gather | solution.py:33
  45.3 6.4 %copy-start.2 = (f32[256,512]{1,0:T(8,128)}, f32[256,512]{1,0:T(8,128)S(1)}, u32[]{:S(2)}) copy-start(f32[256,512]{1,0:T(8,128)S(1)} %fusion.16) | copy-start | bytes 1572868
  45.3 5.6 %copy-start.5 = (bf16[3,3,64,512]{3,2,1,0:T(8,128)(2,1)S(1)}, bf16[3,3,64,512]{3,2,1,0:T(8,128)(2,1)}, u32[]{:S(2)}) copy-start(bf16[3,3,64,512]{3,2,1,0:T(8,128)(2,1)} %param.7) | copy-start | bytes 1769476
  45.5 9.8 %collective-permute-start.1 = (bf16[1,256,512]{2,1,0:T(8,128)(2,1)S(1)}, bf16[1,256,512]{2,1,0:T(8,128)(2,1)S(1)}, u32[]{:S(2)}, u32[]{:S(2)}) collective-permute-start(bf16[1,256,512]{2,1,0:T(8,128)(2,1)S(1)} %fusion.37), channel_id=1, source_target_pairs={{8,0},{16,8},{24,16},{9,1},{17,9},{25,17},{10,2},{18,10},{26,18},{... | collective-permute-start | bytes 786440 | tf_op jit(solution)/shard_map/ppermute | solution.py:20
  46.9 9.1 %collective-permute-start = (bf16[1,256,512]{2,1,0:T(8,128)(2,1)S(1)}, bf16[1,256,512]{2,1,0:T(8,128)(2,1)S(1)}, u32[]{:S(2)}, u32[]{:S(2)}) collective-permute-start(bf16[1,256,512]{2,1,0:T(8,128)(2,1)S(1)} %fusion.37), channel_id=1, source_target_pairs={{0,8},{8,16},{16,24},{1,9},{9,17},{17,25},{2,10},{10,18},{18,26},{... | collective-permute-start | bytes 786440 | tf_op jit(solution)/shard_map/ppermute | solution.py:18
  60.1 84.3 %reduce-scatter.5.cloned.1.call-start = ((), (), s32[]{:S(2)}) async-start(), calls=%async_computation.5 | async-start | bytes 2359296 | tf_op jit(solution)/shard_map/reduce_scatter | solution.py:130
  77.6 7.1 %collective-permute-start.3 = (bf16[1,256,512]{2,1,0:T(8,128)(2,1)S(1)}, bf16[1,256,512]{2,1,0:T(8,128)(2,1)S(1)}, u32[]{:S(2)}, u32[]{:S(2)}) collective-permute-start(bf16[1,256,512]{2,1,0:T(8,128)(2,1)S(1)} %bitcast.285), channel_id=1, source_target_pairs={{8,0},{16,8},{24,16},{9,1},{17,9},{25,17},{10,2},{18,10},{26,18},{... | collective-permute-start | bytes 786440 | tf_op jit(solution)/shard_map/ppermute | solution.py:20
  78.9 7.3 %collective-permute-start.2 = (bf16[1,256,512]{2,1,0:T(8,128)(2,1)S(1)}, bf16[1,256,512]{2,1,0:T(8,128)(2,1)S(1)}, u32[]{:S(2)}, u32[]{:S(2)}) collective-permute-start(bf16[1,256,512]{2,1,0:T(8,128)(2,1)S(1)} %bitcast.286), channel_id=1, source_target_pairs={{0,8},{8,16},{16,24},{1,9},{9,17},{17,25},{2,10},{10,18},{18,26},{... | collective-permute-start | bytes 786440 | tf_op jit(solution)/shard_map/ppermute | solution.py:18
  91.9 2.3 copy-start.3
  94.4 4.9 %copy-start = (bf16[256,512]{1,0:T(8,128)(2,1)}, bf16[256,512]{1,0:T(8,128)(2,1)S(1)}, u32[]{:S(2)}) copy-start(bf16[256,512]{1,0:T(8,128)(2,1)S(1)} %multiply_convert_fusion) | copy-start | bytes 786436
  99.4 75.4 %all-gather.14.cloned.1.call-start = ((), (), s32[]{:S(2)}) async-start(), calls=%async_computation.6 | async-start | bytes 1310720 | tf_op jit(solution)/shard_map/all_gather | solution.py:118
  100.0 164.1 %all-gather.16.cloned.1.call-start = ((), (), s32[]{:S(2)}) async-start(), calls=%async_computation.8 | async-start | bytes 10485760 | tf_op jit(solution)/shard_map/all_gather | solution.py:118
  100.6 192.1 %all-gather.20.cloned.1.call-start = ((), (), s32[]{:S(2)}) async-start(), calls=%async_computation.10 | async-start | bytes 1310720 | tf_op jit(solution)/shard_map/all_gather | solution.py:118
  101.3 280.6 %all-gather.18.cloned.1.call-start = ((), (), s32[]{:S(2)}) async-start(), calls=%async_computation.9 | async-start | bytes 10485760 | tf_op jit(solution)/shard_map/all_gather | solution.py:118
  109.5 321.9 %all-reduce.4.cloned.1.call-start = ((), (), s32[]{:S(2)}) async-start(), calls=%async_computation.7 | async-start | bytes 1179648 | tf_op jit(solution)/shard_map/psum | solution.py:146
  117.8 3.9 copy-start.1
  118.7 3.0 copy-start.6
  121.8 22.6 %copy-start.4 = (bf16[1,256,512]{2,1,0:T(8,128)(2,1)S(1)}, bf16[1,256,512]{2,1,0:T(8,128)(2,1)}, u32[]{:S(2)}) copy-start(bf16[1,256,512]{2,1,0:T(8,128)(2,1)} %param.9) | copy-start | bytes 786436
Sparse Core Ops, SparseCore 0:
  9.6 31.5 all-gather.9
  44.1 32.1 reduce-scatter.2
  78.5 30.9 all-gather.11
  112.2 32.1 reduce-scatter.4
  146.7 28.0 all-gather.13
  176.5 87.5 all-gather.15
  266.0 26.6 all-gather.19
  294.4 87.4 all-gather.17
  385.5 45.8 all-reduce.3

commit v2 on v1

--- a/solution.py
+++ b/solution.py
@@ -1,10 +1,15 @@
 import jax
 import jax.numpy as jnp
 from jax import lax
+from jax.experimental import pallas as pl
+from jax.experimental.pallas import tpu as pltpu
 from jax.sharding import PartitionSpec as P
 
 
 GATHER_BYTES = 8 * 1024 * 1024
+MESH = pl.DeviceIdType.MESH
+BF = jnp.bfloat16
+F32 = jnp.float32
 
 
 def padded_2(cells, sides, width):
@@ -42,7 +47,7 @@
     return local.reshape(local.shape[0], local.shape[1], local.shape[2] // group_width, group_width)
 
 
-def body(features, w_in, w_group, w_out, cotangent):
+def wide_body(features, w_in, w_group, w_out, cotangent):
     row_count, col_count, local_ch = features.shape
     group_width = w_group.shape[2]
     local_mid = w_in.shape[1]
@@ -147,6 +152,456 @@
     return block_out, grad_input, in_grad, group_grad, out_grad
 
 
+def dot(a, b):
+    return jnp.dot(a, b, preferred_element_type=F32)
+
+
+def dot_nt(a, b):
+    return lax.dot_general(a, b, (((1,), (1,)), ((), ())), preferred_element_type=F32)
+
+
+def dot_tn(a, b):
+    return lax.dot_general(a, b, (((0,), (0,)), ((), ())), preferred_element_type=F32)
+
+
+def moved(values, step):
+    count = values.shape[0]
+    at = lax.broadcasted_iota(jnp.int32, values.shape, 0)
+    edge = 0 if step == 1 else count - 1
+    return jnp.where(at == edge, 0.0, pltpu.roll(values, step % count, 0))
+
+
+class Fabric:
+    def __init__(self):
+        self.row = lax.axis_index("row")
+        self.ch = lax.axis_index("ch")
+        self.core = lax.rem(self.ch, 2)
+        self.z = self.ch // 2
+        self.zs = lax.axis_size("ch") // 2
+        x, y = lax.rem(self.row, 2), self.row // 2
+        self.row_x = y * 2 + (1 - x)
+        self.row_y = (1 - y) * 2 + x
+        self.row_d = (1 - y) * 2 + (1 - x)
+        self.twin = self.z * 2 + (1 - self.core)
+        self.sent = []
+
+    def z_at(self, d):
+        return lax.rem(self.z + d, self.zs)
+
+    def ch_at(self, d):
+        return self.z_at(d) * 2 + self.core
+
+    def partners(self):
+        out = [(self.row, self.ch_at(d)) for d in range(1, self.zs)]
+        out += [(r, self.ch) for r in (self.row_x, self.row_y, self.row_d)]
+        return out + [(self.row, self.twin)]
+
+    def send(self, src, dst, send_sem, recv_sem, device):
+        copy = pltpu.make_async_remote_copy(
+            src_ref=src,
+            dst_ref=dst,
+            send_sem=send_sem,
+            recv_sem=recv_sem,
+            device_id=device,
+            device_id_type=MESH,
+        )
+        copy.start()
+        self.sent.append(copy)
+
+    def arrived(self, dst, sem):
+        pltpu.make_async_remote_copy(
+            src_ref=dst,
+            dst_ref=dst,
+            send_sem=sem,
+            recv_sem=sem,
+            device_id=(self.row, self.twin),
+            device_id_type=MESH,
+        ).wait_recv()
+
+
+class Gather:
+    def __init__(self, fab, buf, recv, send_z, send_x, send_y, send_t):
+        self.fab, self.buf, self.recv = fab, buf, recv
+        self.send_z, self.send_x, self.send_y, self.send_t = send_z, send_x, send_y, send_t
+
+    def push(self, k, r, send_sem, device):
+        slot = self.buf.at[k, r]
+        self.fab.send(slot, slot, send_sem, self.recv.at[k, r], device)
+
+    def to_x(self, k, r, n):
+        self.push(k, r, self.send_x.at[n], (self.fab.row_x, self.fab.ch))
+
+    def to_y(self, k, r, n):
+        self.push(k, r, self.send_y.at[n], (self.fab.row_y, self.fab.ch))
+
+    def to_twin(self, k, r, n):
+        self.push(k, r, self.send_t.at[n], (self.fab.row, self.fab.twin))
+
+    def wait(self, k, r):
+        self.fab.arrived(self.buf.at[k, r], self.recv.at[k, r])
+
+    def start(self):
+        f = self.fab
+        for d in range(1, f.zs):
+            self.push(f.ch, f.row, self.send_z.at[d - 1], (f.row, f.ch_at(d)))
+        self.to_x(f.ch, f.row, 0)
+        self.to_y(f.ch, f.row, 0)
+        self.to_twin(f.ch, f.row, 0)
+
+    def pump_z(self):
+        f = self.fab
+        for d in range(1, f.zs):
+            k = f.ch_at(d)
+            self.wait(k, f.row)
+            self.to_x(k, f.row, d)
+            self.to_y(k, f.row, d)
+            self.to_twin(k, f.row, d)
+
+    def pump_xy(self):
+        f = self.fab
+        half = f.zs // 2
+        for d in range(f.zs):
+            k = f.ch_at(d)
+            self.wait(k, f.row_x)
+            if d < half:
+                self.to_y(k, f.row_x, f.zs + d)
+            self.to_twin(k, f.row_x, f.zs + d)
+            self.wait(k, f.row_y)
+            if d >= half:
+                self.to_x(k, f.row_y, f.zs + d - half)
+            self.to_twin(k, f.row_y, 2 * f.zs + d)
+
+    def pump_d(self):
+        f = self.fab
+        for d in range(f.zs):
+            k = f.ch_at(d)
+            self.wait(k, f.row_d)
+            self.to_twin(k, f.row_d, 3 * f.zs + d)
+
+    def twin_row(self, r):
+        f = self.fab
+        for d in range(f.zs):
+            self.wait(f.z_at(d) * 2 + (1 - f.core), r)
+
+
+class Scatter:
+    def __init__(self, fab, give, got, out, far, acc, give_s, got_s, out_s, far_s):
+        self.fab, self.give, self.got, self.out, self.far, self.acc = fab, give, got, out, far, acc
+        self.give_s, self.got_s, self.out_s, self.far_s = give_s, got_s, out_s, far_s
+
+    def part(self, lhs, w_ref, k):
+        width = lhs.shape[1]
+        rows = pl.ds(pl.multiple_of(k * width, width), width)
+        return dot_nt(lhs, w_ref[rows, :])
+
+    def start(self, lhs, w_ref):
+        f = self.fab
+        for d in (1, 2, 3, 0):
+            at = f.z_at(d)
+            self.give[at] = self.part(lhs, w_ref, at * 2 + (1 - f.core)).astype(BF)
+            f.send(
+                self.give.at[at],
+                self.got.at[at],
+                self.give_s.at[d],
+                self.got_s.at[at],
+                (f.row, f.twin),
+            )
+
+    def middle(self, lhs, w_ref):
+        f = self.fab
+        for d in (1, 2, 3, 0):
+            at = f.z_at(d)
+            own = self.part(lhs, w_ref, at * 2 + f.core)
+            f.arrived(self.got.at[at], self.got_s.at[at])
+            own = own + self.got[at].astype(F32)
+            if d == 0:
+                self.acc[...] = own
+            else:
+                self.out[at] = own.astype(BF)
+                f.send(
+                    self.out.at[at],
+                    self.far.at[f.z],
+                    self.out_s.at[d - 1],
+                    self.far_s.at[f.z],
+                    (f.row, f.ch_at(d)),
+                )
+
+    def finish(self):
+        f = self.fab
+        for d in (1, 2, 3):
+            at = f.z_at(d)
+            f.arrived(self.far.at[at], self.far_s.at[at])
+        total = self.acc[...]
+        for d in (1, 2, 3):
+            total = total + self.far[f.z_at(d)].astype(F32)
+        return total
+
+
+def block_kernel(*refs):
+    (feat, w_in_hbm, wg, w_out_hbm, cot, out, g_in, gw_in, gw_group, gw_out) = refs[:10]
+    (b1, b2, w_in, w_out, pre, act, gt, g1, cots, shifted, wide, stage) = refs[10:22]
+    (r1, z1, x1, y1, t1, r2, z2, x2, y2, t2) = refs[22:32]
+    s1, s2 = refs[32:41], refs[41:50]
+    cot_send, cot_recv, gt_send, gt_recv, local = refs[50:55]
+    fab = Fabric()
+    rows = cots.shape[0]
+    pixels, width = feat.shape
+    chunk = wide.shape[2]
+    gw = wg.shape[1]
+    count_k = b1.shape[0]
+    chunks = [slice(i * chunk, (i + 1) * chunk) for i in range(width // chunk)]
+
+    load_out = pltpu.make_async_copy(w_out_hbm, w_out, local.at[0])
+    load_in = pltpu.make_async_copy(w_in_hbm, w_in, local.at[1])
+    load_out.start()
+    load_in.start()
+    barrier = pltpu.get_barrier_semaphore()
+    partners = fab.partners()
+    for device in partners:
+        pl.semaphore_signal(barrier, inc=1, device_id=device, device_id_type=MESH)
+    pl.semaphore_wait(barrier, len(partners))
+
+    gather1 = Gather(fab, b1, r1, z1, x1, y1, t1)
+    gather2 = Gather(fab, b2, r2, z2, x2, y2, t2)
+    scatter1 = Scatter(fab, *s1)
+    scatter2 = Scatter(fab, *s2)
+    other_rows = (fab.row_x, fab.row_y, fab.row_d)
+
+    b1[fab.ch, fab.row] = feat[...]
+    gather1.start()
+    cots[fab.row] = cot[...]
+    load_out.wait()
+    scatter1.start(cot[...], w_out)
+
+    blank = jnp.zeros((pixels, width), BF)
+    act[0] = blank
+    act[rows + 1] = blank
+    gt[0] = blank
+    gt[rows + 1] = blank
+    row_group = lax.broadcasted_iota(jnp.int32, (chunk, chunk), 0) // gw
+    col_group = lax.broadcasted_iota(jnp.int32, (chunk, chunk), 1) // gw
+    same = row_group == col_group
+
+    def widen(tap, carry):
+        for i, part in enumerate(chunks):
+            taps = wg[tap, :, part].astype(F32)
+            dense = jnp.concatenate([taps] * (chunk // gw), axis=0)
+            wide[tap, i] = jnp.where(same, dense, 0.0).astype(BF)
+        return carry
+
+    lax.fori_loop(0, 9, widen, 0)
+
+    scatter1.middle(cot[...], w_out)
+    gather1.pump_z()
+    for n, r in enumerate(other_rows):
+        fab.send(
+            cots.at[fab.row],
+            cots.at[fab.row],
+            cot_send.at[n],
+            cot_recv.at[fab.row],
+            (r, fab.ch),
+        )
+    load_in.wait()
+
+    def first(r):
+        gather1.twin_row(r)
+        pre[r] = jnp.zeros((pixels, width), F32)
+
+        def add(k, carry):
+            lines = pl.ds(pl.multiple_of(k * width, width), width)
+            pre[r] += dot(b1[k, r], w_in[lines, :])
+            return carry
+
+        lax.fori_loop(0, count_k, add, 0)
+        value = pre[r]
+        act[r + 1] = (value * jax.nn.sigmoid(value)).astype(BF)
+
+    first(fab.row)
+    gather1.pump_xy()
+    first(fab.row_x)
+    gather1.pump_d()
+    first(fab.row_d)
+    first(fab.row_y)
+
+    taps_of = [[a * 3 + b for a in range(3)] for b in range(3)]
+    two = []
+    for i, part in enumerate(chunks):
+        total = None
+        for b in range(3):
+            side = None
+            for a in range(3):
+                term = dot(act[fab.row + a, :, part], wide[taps_of[b][a], i])
+                side = term if side is None else side + term
+            side = moved(side, 1) if b == 0 else moved(side, -1) if b == 2 else side
+            total = side if total is None else total + side
+        two.append(total)
+    slopes = []
+    for i, part in enumerate(chunks):
+        b2[fab.ch, fab.row, :, part] = (two[i] * jax.nn.sigmoid(two[i])).astype(BF)
+        slopes.append(silu_slope(two[i]))
+    gather2.start()
+    d_two = scatter1.finish()
+    for i, part in enumerate(chunks):
+        gt[fab.row + 1, :, part] = (d_two[:, part] * slopes[i]).astype(BF)
+    for n, r in enumerate(other_rows):
+        fab.send(
+            gt.at[fab.row + 1],
+            gt.at[fab.row + 1],
+            gt_send.at[n],
+            gt_recv.at[fab.row],
+            (r, fab.ch),
+        )
+    gather2.pump_z()
+    for r in other_rows:
+        fab.arrived(gt.at[r + 1], gt_recv.at[r])
+
+    def back(q, carry):
+        for i, part in enumerate(chunks):
+            total = None
+            for b in range(3):
+                side = None
+                for a in range(3):
+                    term = dot_nt(gt[q + 2 - a, :, part], wide[taps_of[b][a], i])
+                    side = term if side is None else side + term
+                side = moved(side, -1) if b == 0 else moved(side, 1) if b == 2 else side
+                total = side if total is None else total + side
+            g1[q, :, part] = (total * silu_slope(pre[q, :, part])).astype(BF)
+        return carry
+
+    lax.fori_loop(0, rows, back, 0)
+    scatter2.start(g1[fab.row], w_in)
+    scatter2.middle(g1[fab.row], w_in)
+    gather2.pump_xy()
+
+    gather2.twin_row(fab.row)
+    pre[0] = feat[...].astype(F32)
+
+    def last(k, carry):
+        lines = pl.ds(pl.multiple_of(k * width, width), width)
+        pre[0] += dot(b2[k, fab.row], w_out[lines, :])
+        return carry
+
+    lax.fori_loop(0, count_k, last, 0)
+    out[...] = pre[0].astype(BF)
+
+    def weight_grad(left, right, result, sems):
+        def store(k, slot):
+            return pltpu.make_async_copy(
+                stage.at[slot],
+                result.at[pl.ds(pl.multiple_of(k * width, width), width), :],
+                sems.at[slot],
+            )
+
+        def step(pair, carry):
+            for slot in range(2):
+                k = pair * 2 + slot
+
+                @pl.when(pair > 0)
+                def _():
+                    store(k - 2, slot).wait()
+
+                lhs = left[k].reshape(rows * pixels, width)
+                stage[slot] = dot_tn(lhs, right[...].reshape(rows * pixels, width)).astype(BF)
+                store(k, slot).start()
+            return carry
+
+        lax.fori_loop(0, count_k // 2, step, 0)
+        for slot in range(2):
+            store(count_k - 2 + slot, slot).wait()
+
+    weight_grad(b1, g1, gw_in, local.at[pl.ds(2, 2)])
+    gather2.pump_d()
+
+    for b in range(3):
+
+        def move(q, carry):
+            value = gt[q + 1].astype(F32)
+            value = moved(value, -1) if b == 0 else moved(value, 1) if b == 2 else value
+            shifted[q] = value.astype(BF)
+            return carry
+
+        lax.fori_loop(0, rows, move, 0)
+
+        def tap_grad(a, carry):
+            for part in chunks:
+                lhs = act[pl.ds(a, rows), :, part].reshape(rows * pixels, chunk)
+                full = dot_tn(lhs, shifted[:, :, part].reshape(rows * pixels, chunk))
+                full = jnp.where(same, full, 0.0).reshape(chunk // gw, gw, chunk)
+                gw_group[a * 3 + b, :, part] = jnp.sum(full, axis=0).astype(BF)
+            return carry
+
+        lax.fori_loop(0, 3, tap_grad, 0)
+
+    g_in[...] = (cot[...].astype(F32) + scatter2.finish()).astype(BF)
+    for r in other_rows:
+        fab.arrived(cots.at[r], cot_recv.at[r])
+        gather2.twin_row(r)
+    weight_grad(b2, cots, gw_out, local.at[pl.ds(4, 2)])
+    for copy in fab.sent:
+        copy.wait_send()
+
+
+def body(features, w_in, w_group, w_out, cotangent):
+    row_count, pixels, width = features.shape
+    rows, lanes = lax.axis_size("row"), lax.axis_size("ch")
+    total = rows * lanes * features.size * features.dtype.itemsize
+    fits = (rows, lanes, row_count) == (4, 8, 1) and w_in.shape[1] == width == 512
+    if not fits or total > GATHER_BYTES:
+        return wide_body(features, w_in, w_group, w_out, cotangent)
+    zs = lanes // 2
+    channels = w_in.shape[0]
+    gw = w_group.shape[2]
+    dma = pltpu.SemaphoreType.DMA
+    vmem = pltpu.VMEM
+    gather_sems = [dma((lanes, rows)), dma((zs - 1,)), dma((6,)), dma((6,)), dma((rows * zs,))]
+    part = vmem((zs, pixels, width), BF)
+    scatter = [part, part, part, part, vmem((pixels, width), F32)]
+    scatter += [dma((zs,)), dma((zs,)), dma((zs - 1,)), dma((zs,))]
+    scratch = [
+        vmem((lanes, rows, pixels, width), BF),
+        vmem((lanes, rows, pixels, width), BF),
+        vmem((channels, width), BF),
+        vmem((channels, width), BF),
+        vmem((rows, pixels, width), F32),
+        vmem((rows + 2, pixels, width), BF),
+        vmem((rows + 2, pixels, width), BF),
+        vmem((rows, pixels, width), BF),
+        vmem((rows, pixels, width), BF),
+        vmem((rows, pixels, width), BF),
+        vmem((9, width // 256, 256, 256), BF),
+        vmem((2, width, width), BF),
+    ]
+    scratch += gather_sems * 2 + scatter * 2
+    scratch += [dma((3,)), dma((rows,)), dma((3,)), dma((rows,)), dma((6,))]
+    in_vmem = pl.BlockSpec(memory_space=pltpu.VMEM)
+    in_any = pl.BlockSpec(memory_space=pl.ANY)
+    flat = jax.ShapeDtypeStruct((pixels, width), BF)
+    weight = jax.ShapeDtypeStruct((channels, width), BF)
+    out, g_in, gw_in, gw_group, gw_out = pl.pallas_call(
+        block_kernel,
+        out_shape=[flat, flat, weight, jax.ShapeDtypeStruct((9, gw, width), BF), weight],
+        in_specs=[in_vmem, in_any, in_vmem, in_any, in_vmem],
+        out_specs=[in_vmem, in_vmem, in_any, in_vmem, in_any],
+        scratch_shapes=scratch,
+        compiler_params=pltpu.CompilerParams(
+            collective_id=0, has_side_effects=True, vmem_limit_bytes=60 * 1024 * 1024
+        ),
+    )(
+        features.reshape(pixels, width),
+        w_in,
+        w_group.reshape(9, gw, width),
+        w_out,
+        cotangent.reshape(pixels, width),
+    )
+    return (
+        out.reshape(features.shape),
+        g_in.reshape(features.shape),
+        gw_in,
+        gw_group.reshape(w_group.shape),
+        gw_out,
+    )
+
+
 def solution(mesh):
     placed = (
         P("row", None, "ch"),

time: 441 us -> 161 us (0.37)
  the two profiles are of different devices: /device:TPU:1 before, /device:TPU:9 now
where the time goes in v2:
time: 161 us; the launch traced here: 160 us
  Pallas kernels  149 us (93%)
  local copies, waits for them, and re-layouts  10.8 us (7%)
    pallas_call x1, Pallas kernels, body(): pl.pallas_call(block_kernel, out_shape=[flat, flat, weight, jax.ShapeDtyp...  149 us
    unnamed x9, local copies, waits for them, and re-layouts  10.8 us

profile of v2, /device:TPU:9, one launch (start us, length us, event | category | flops | bytes accessed | tf_op | source)
XLA Modules:
  0.0 160.4 jit_solution(7049163670392133489)
XLA Ops:
  0.6 148.9 %shard_map.92 = (bf16[256,512]{1,0:T(8,128)(2,1)}, bf16[256,512]{1,0:T(8,128)(2,1)}, bf16[4096,512]{1,0:T(8,128)(2,1)}, bf16[9,64,512]{2,1,0:T(8,128)(2,1)}, bf16[4096,512]{1,0:T(8,128)(2,1)}) custom-call(bf16[256,512]{1,0:T(8,128)(2,1)} %bitcast.8, bf16[4096,512]{1,0:T(8,128)(2,1)} %refs_1_.1, bf16[9,64,512]{2,1,0:T(8,128)(2,1)} %bitcast.6, ...), custom_call_target="tpu_custom_call" | custom-call | tf_op jit(solution)/shard_map/pallas_call | solution.py:580
  149.5 1.7 %copy.15 = bf16[1,256,512]{2,1,0:T(8,128)(2,1)} copy(bf16[1,256,512]{2,1,0:T(8,128)(2,1)} %bitcast.11) | data formatting | bytes 524288
  151.2 1.7 %copy.16 = bf16[1,256,512]{2,1,0:T(8,128)(2,1)} copy(bf16[1,256,512]{2,1,0:T(8,128)(2,1)} %bitcast.10) | data formatting | bytes 524288
  152.9 0.0 copy-start.1
  152.9 0.0 copy-start
  152.9 4.6 %copy.17 = bf16[4096,512]{1,0:T(8,128)(2,1)} copy(bf16[4096,512]{1,0:T(8,128)(2,1)} %get-tuple-element.22) | data formatting | bytes 8388608
  157.5 0.0 copy-done.1
  157.5 0.8 copy.18
  158.3 0.0 copy-done
  158.3 2.0 %copy.19 = bf16[4096,512]{1,0:T(8,128)(2,1)} copy(bf16[4096,512]{1,0:T(8,128)(2,1)S(1)} %copy-done) | data formatting | bytes 8388608
Async XLA Ops:
  152.9 4.6 %copy-start.1 = (bf16[9,64,512]{2,1,0:T(8,128)(2,1)S(1)}, bf16[9,64,512]{2,1,0:T(8,128)(2,1)}, u32[]{:S(2)}) copy-start(bf16[9,64,512]{2,1,0:T(8,128)(2,1)} %get-tuple-element.13) | copy-start | bytes 1769476
  152.9 5.5 %copy-start = (bf16[4096,512]{1,0:T(8,128)(2,1)S(1)}, bf16[4096,512]{1,0:T(8,128)(2,1)}, u32[]{:S(2)}) copy-start(bf16[4096,512]{1,0:T(8,128)(2,1)} %get-tuple-element.24) | copy-start | bytes 12582916

commit v3 on v2

--- a/solution.py
+++ b/solution.py
@@ -248,40 +248,38 @@
         self.to_y(f.ch, f.row, 0)
         self.to_twin(f.ch, f.row, 0)
 
-    def pump_z(self):
-        f = self.fab
-        for d in range(1, f.zs):
-            k = f.ch_at(d)
-            self.wait(k, f.row)
-            self.to_x(k, f.row, d)
-            self.to_y(k, f.row, d)
-            self.to_twin(k, f.row, d)
-
-    def pump_xy(self):
+    def land_z(self, d):
+        f = self.fab
+        self.wait(f.ch_at(d), f.row)
+        self.to_twin(f.ch_at(d), f.row, d)
+
+    def spread_z(self, d):
+        f = self.fab
+        self.to_x(f.ch_at(d), f.row, d)
+        self.to_y(f.ch_at(d), f.row, d)
+
+    def pump_xy(self, d):
         f = self.fab
         half = f.zs // 2
-        for d in range(f.zs):
-            k = f.ch_at(d)
-            self.wait(k, f.row_x)
-            if d < half:
-                self.to_y(k, f.row_x, f.zs + d)
-            self.to_twin(k, f.row_x, f.zs + d)
-            self.wait(k, f.row_y)
-            if d >= half:
-                self.to_x(k, f.row_y, f.zs + d - half)
-            self.to_twin(k, f.row_y, 2 * f.zs + d)
-
-    def pump_d(self):
-        f = self.fab
-        for d in range(f.zs):
-            k = f.ch_at(d)
-            self.wait(k, f.row_d)
-            self.to_twin(k, f.row_d, 3 * f.zs + d)
-
-    def twin_row(self, r):
-        f = self.fab
-        for d in range(f.zs):
-            self.wait(f.z_at(d) * 2 + (1 - f.core), r)
+        k = f.ch_at(d)
+        self.wait(k, f.row_x)
+        if d < half:
+            self.to_y(k, f.row_x, f.zs + d)
+        self.to_twin(k, f.row_x, f.zs + d)
+        self.wait(k, f.row_y)
+        if d >= half:
+            self.to_x(k, f.row_y, f.zs + d - half)
+        self.to_twin(k, f.row_y, 2 * f.zs + d)
+
+    def pump_d(self, d):
+        f = self.fab
+        k = f.ch_at(d)
+        self.wait(k, f.row_d)
+        self.to_twin(k, f.row_d, 3 * f.zs + d)
+
+    def from_twin(self, d, r):
+        f = self.fab
+        self.wait(f.z_at(d) * 2 + (1 - f.core), r)
 
 
 class Scatter:
@@ -342,7 +340,7 @@
     (b1, b2, w_in, w_out, pre, act, gt, g1, cots, shifted, wide, stage) = refs[10:22]
     (r1, z1, x1, y1, t1, r2, z2, x2, y2, t2) = refs[22:32]
     s1, s2 = refs[32:41], refs[41:50]
-    cot_send, cot_recv, gt_send, gt_recv, local = refs[50:55]
+    cot_send, cot_recv, gt_send, gt_recv, halo_send, halo_recv, local = refs[50:57]
     fab = Fabric()
     rows = cots.shape[0]
     pixels, width = feat.shape
@@ -370,6 +368,14 @@
     b1[fab.ch, fab.row] = feat[...]
     gather1.start()
     cots[fab.row] = cot[...]
+    for n, r in enumerate(other_rows):
+        fab.send(
+            cots.at[fab.row],
+            cots.at[fab.row],
+            cot_send.at[n],
+            cot_recv.at[fab.row],
+            (r, fab.ch),
+        )
     load_out.wait()
     scatter1.start(cot[...], w_out)
 
@@ -391,20 +397,12 @@
 
     lax.fori_loop(0, 9, widen, 0)
 
-    scatter1.middle(cot[...], w_out)
-    gather1.pump_z()
-    for n, r in enumerate(other_rows):
-        fab.send(
-            cots.at[fab.row],
-            cots.at[fab.row],
-            cot_send.at[n],
-            cot_recv.at[fab.row],
-            (r, fab.ch),
-        )
+    depths = range(fab.zs)
     load_in.wait()
 
     def first(r):
-        gather1.twin_row(r)
+        for d in depths:
+            gather1.from_twin(d, r)
         pre[r] = jnp.zeros((pixels, width), F32)
 
         def add(k, carry):
@@ -416,12 +414,52 @@
         value = pre[r]
         act[r + 1] = (value * jax.nn.sigmoid(value)).astype(BF)
 
+    for d in depths[1:]:
+        gather1.land_z(d)
     first(fab.row)
-    gather1.pump_xy()
-    first(fab.row_x)
-    gather1.pump_d()
-    first(fab.row_d)
-    first(fab.row_y)
+    above, below = fab.row > 0, fab.row < rows - 1
+
+    def halo(n, r):
+        return pltpu.make_async_remote_copy(
+            src_ref=act.at[fab.row + 1],
+            dst_ref=act.at[fab.row + 1],
+            send_sem=halo_send.at[n],
+            recv_sem=halo_recv.at[n],
+            device_id=(r, fab.ch),
+            device_id_type=MESH,
+        )
+
+    def halo_from(n, r):
+        return pltpu.make_async_remote_copy(
+            src_ref=act.at[r + 1],
+            dst_ref=act.at[r + 1],
+            send_sem=halo_send.at[n],
+            recv_sem=halo_recv.at[n],
+            device_id=(r, fab.ch),
+            device_id_type=MESH,
+        )
+
+    @pl.when(above)
+    def _():
+        halo(0, fab.row - 1).start()
+
+    @pl.when(below)
+    def _():
+        halo(1, fab.row + 1).start()
+
+    for d in depths[1:]:
+        gather1.spread_z(d)
+    scatter1.middle(cot[...], w_out)
+
+    @pl.when(above)
+    def _():
+        halo(0, fab.row - 1).wait_send()
+        halo_from(1, fab.row - 1).wait_recv()
+
+    @pl.when(below)
+    def _():
+        halo(1, fab.row + 1).wait_send()
+        halo_from(0, fab.row + 1).wait_recv()
 
     taps_of = [[a * 3 + b for a in range(3)] for b in range(3)]
     two = []
@@ -440,6 +478,10 @@
         b2[fab.ch, fab.row, :, part] = (two[i] * jax.nn.sigmoid(two[i])).astype(BF)
         slopes.append(silu_slope(two[i]))
     gather2.start()
+    for d in depths:
+        gather1.pump_xy(d)
+    first(fab.row_x)
+    first(fab.row_y)
     d_two = scatter1.finish()
     for i, part in enumerate(chunks):
         gt[fab.row + 1, :, part] = (d_two[:, part] * slopes[i]).astype(BF)
@@ -451,7 +493,12 @@
             gt_recv.at[fab.row],
             (r, fab.ch),
         )
-    gather2.pump_z()
+    for d in depths:
+        gather1.pump_d(d)
+    for d in depths[1:]:
+        gather2.land_z(d)
+        gather2.spread_z(d)
+    first(fab.row_d)
     for r in other_rows:
         fab.arrived(gt.at[r + 1], gt_recv.at[r])
 
@@ -471,9 +518,9 @@
     lax.fori_loop(0, rows, back, 0)
     scatter2.start(g1[fab.row], w_in)
     scatter2.middle(g1[fab.row], w_in)
-    gather2.pump_xy()
-
-    gather2.twin_row(fab.row)
+
+    for d in depths:
+        gather2.from_twin(d, fab.row)
     pre[0] = feat[...].astype(F32)
 
     def last(k, carry):
@@ -484,33 +531,33 @@
     lax.fori_loop(0, count_k, last, 0)
     out[...] = pre[0].astype(BF)
 
-    def weight_grad(left, right, result, sems):
-        def store(k, slot):
+    def weight_grad(left, right, result, sems, d):
+        def store(slot):
+            k = fab.z_at(d) * 2 + slot
             return pltpu.make_async_copy(
                 stage.at[slot],
                 result.at[pl.ds(pl.multiple_of(k * width, width), width), :],
                 sems.at[slot],
             )
 
-        def step(pair, carry):
+        def step(slot, carry):
+            lhs = left[fab.z_at(d) * 2 + slot].reshape(rows * pixels, width)
+            rhs = right[...].reshape(rows * pixels, width)
+            full = dot_tn(lhs, rhs).astype(BF)
+            if d > 0:
+                store(slot).wait()
+            stage[slot] = full
+            store(slot).start()
+            return carry
+
+        lax.fori_loop(0, 2, step, 0)
+        if d == fab.zs - 1:
             for slot in range(2):
-                k = pair * 2 + slot
-
-                @pl.when(pair > 0)
-                def _():
-                    store(k - 2, slot).wait()
-
-                lhs = left[k].reshape(rows * pixels, width)
-                stage[slot] = dot_tn(lhs, right[...].reshape(rows * pixels, width)).astype(BF)
-                store(k, slot).start()
-            return carry
-
-        lax.fori_loop(0, count_k // 2, step, 0)
-        for slot in range(2):
-            store(count_k - 2 + slot, slot).wait()
-
-    weight_grad(b1, g1, gw_in, local.at[pl.ds(2, 2)])
-    gather2.pump_d()
+                store(slot).wait()
+
+    for d in depths:
+        weight_grad(b1, g1, gw_in, local.at[pl.ds(2, 2)], d)
+        gather2.pump_xy(d)
 
     for b in range(3):
 
@@ -535,8 +582,11 @@
     g_in[...] = (cot[...].astype(F32) + scatter2.finish()).astype(BF)
     for r in other_rows:
         fab.arrived(cots.at[r], cot_recv.at[r])
-        gather2.twin_row(r)
-    weight_grad(b2, cots, gw_out, local.at[pl.ds(4, 2)])
+    for d in depths:
+        gather2.pump_d(d)
+        for r in other_rows:
+            gather2.from_twin(d, r)
+        weight_grad(b2, cots, gw_out, local.at[pl.ds(4, 2)], d)
     for copy in fab.sent:
         copy.wait_send()
 
@@ -572,7 +622,7 @@
         vmem((2, width, width), BF),
     ]
     scratch += gather_sems * 2 + scatter * 2
-    scratch += [dma((3,)), dma((rows,)), dma((3,)), dma((rows,)), dma((6,))]
+    scratch += [dma((3,)), dma((rows,)), dma((3,)), dma((rows,)), dma((2,)), dma((2,)), dma((6,))]
     in_vmem = pl.BlockSpec(memory_space=pltpu.VMEM)
     in_any = pl.BlockSpec(memory_space=pl.ANY)
     flat = jax.ShapeDtypeStruct((pixels, width), BF)

time: 161 us -> 146 us (0.907)
  the two profiles are of different devices: /device:TPU:9 before, /device:TPU:26 now
where the time goes in v3:
time: 146 us
  Pallas kernels  134 us (92%)
  local copies, waits for them, and re-layouts  10.8 us (7%)
    pallas_call x1, Pallas kernels, body(): pl.pallas_call(block_kernel, out_shape=[flat, flat, weight, jax.ShapeDtyp...  134 us
    unnamed x9, local copies, waits for them, and re-layouts  10.8 us

profile of v3, /device:TPU:26, one launch (start us, length us, event | category | flops | bytes accessed | tf_op | source)
XLA Modules:
  0.0 145.8 jit_solution(14651590410855230025)
XLA Ops:
  0.6 134.3 %shard_map.92 = (bf16[256,512]{1,0:T(8,128)(2,1)}, bf16[256,512]{1,0:T(8,128)(2,1)}, bf16[4096,512]{1,0:T(8,128)(2,1)}, bf16[9,64,512]{2,1,0:T(8,128)(2,1)}, bf16[4096,512]{1,0:T(8,128)(2,1)}) custom-call(bf16[256,512]{1,0:T(8,128)(2,1)} %bitcast.8, bf16[4096,512]{1,0:T(8,128)(2,1)} %refs_1_.1, bf16[9,64,512]{2,1,0:T(8,128)(2,1)} %bitcast.6, ...), custom_call_target="tpu_custom_call" | custom-call | tf_op jit(solution)/shard_map/pallas_call | solution.py:630
  135.0 1.7 %copy.15 = bf16[1,256,512]{2,1,0:T(8,128)(2,1)} copy(bf16[1,256,512]{2,1,0:T(8,128)(2,1)} %bitcast.11) | data formatting | bytes 524288
  136.7 1.7 %copy.16 = bf16[1,256,512]{2,1,0:T(8,128)(2,1)} copy(bf16[1,256,512]{2,1,0:T(8,128)(2,1)} %bitcast.10) | data formatting | bytes 524288
  138.3 0.0 copy-start.1
  138.3 0.0 copy-start
  138.3 4.6 %copy.17 = bf16[4096,512]{1,0:T(8,128)(2,1)} copy(bf16[4096,512]{1,0:T(8,128)(2,1)} %get-tuple-element.22) | data formatting | bytes 8388608
  143.0 0.0 copy-done.1
  143.0 0.8 copy.18
  143.8 0.0 copy-done
  143.8 2.0 %copy.19 = bf16[4096,512]{1,0:T(8,128)(2,1)} copy(bf16[4096,512]{1,0:T(8,128)(2,1)S(1)} %copy-done) | data formatting | bytes 8388608
Async XLA Ops:
  138.3 4.6 %copy-start.1 = (bf16[9,64,512]{2,1,0:T(8,128)(2,1)S(1)}, bf16[9,64,512]{2,1,0:T(8,128)(2,1)}, u32[]{:S(2)}) copy-start(bf16[9,64,512]{2,1,0:T(8,128)(2,1)} %get-tuple-element.13) | copy-start | bytes 1769476
  138.3 5.5 %copy-start = (bf16[4096,512]{1,0:T(8,128)(2,1)S(1)}, bf16[4096,512]{1,0:T(8,128)(2,1)}, u32[]{:S(2)}) copy-start(bf16[4096,512]{1,0:T(8,128)(2,1)} %get-tuple-element.24) | copy-start | bytes 12582916

commit v4 on v3

--- a/solution.py
+++ b/solution.py
@@ -184,6 +184,7 @@
         self.row_d = (1 - y) * 2 + (1 - x)
         self.twin = self.z * 2 + (1 - self.core)
         self.sent = []
+        self.held = []
 
     def z_at(self, d):
         return lax.rem(self.z + d, self.zs)
@@ -242,16 +243,69 @@
 
     def start(self):
         f = self.fab
-        for d in range(1, f.zs):
-            self.push(f.ch, f.row, self.send_z.at[d - 1], (f.row, f.ch_at(d)))
+        self.relay(0, 1)
+        self.relay(0, -1)
         self.to_x(f.ch, f.row, 0)
         self.to_y(f.ch, f.row, 0)
         self.to_twin(f.ch, f.row, 0)
 
-    def land_z(self, d):
-        f = self.fab
-        self.wait(f.ch_at(d), f.row)
-        self.to_twin(f.ch_at(d), f.row, d)
+    def relay(self, d, way):
+        f = self.fab
+        k = f.ch_at(d)
+        slot = self.buf.at[k, f.row]
+        sem = self.send_z.at[f.zs if d == 0 and way == 1 else d]
+
+        def copy():
+            return pltpu.make_async_remote_copy(
+                src_ref=slot,
+                dst_ref=slot,
+                send_sem=sem,
+                recv_sem=self.recv.at[k, f.row],
+                device_id=(f.row, f.ch + 2 * way),
+                device_id_type=MESH,
+            )
+
+        above = f.z + d < f.zs
+        came = True if d == 0 else above if way == -1 else jnp.logical_not(above)
+        more = f.z > 0 if way == -1 else f.z < f.zs - 1
+        go = more if d == 0 else jnp.logical_and(came, more)
+
+        @pl.when(go)
+        def _():
+            copy().start()
+
+        f.held.append((go, copy))
+
+    def land_z(self, step):
+        f = self.fab
+        for d, way in ((step, -1), (f.zs - step, 1)):
+            here = f.z + d < f.zs if way == -1 else f.z + d >= f.zs
+
+            @pl.when(here)
+            def _():
+                self.wait(f.ch_at(d), f.row)
+
+            self.relay(d, way)
+
+            @pl.when(here)
+            def _():
+                self.twin_copy(d).start()
+
+    def twin_copy(self, d):
+        f = self.fab
+        slot = self.buf.at[f.ch_at(d), f.row]
+        return pltpu.make_async_remote_copy(
+            src_ref=slot,
+            dst_ref=slot,
+            send_sem=self.send_t.at[d],
+            recv_sem=self.recv.at[f.ch_at(d), f.row],
+            device_id=(f.row, f.twin),
+            device_id_type=MESH,
+        )
+
+    def landed_z(self):
+        for d in range(1, self.fab.zs):
+            self.fab.sent.append(self.twin_copy(d))
 
     def spread_z(self, d):
         f = self.fab
@@ -416,6 +470,7 @@
 
     for d in depths[1:]:
         gather1.land_z(d)
+    gather1.landed_z()
     first(fab.row)
     above, below = fab.row > 0, fab.row < rows - 1
 
@@ -478,10 +533,12 @@
         b2[fab.ch, fab.row, :, part] = (two[i] * jax.nn.sigmoid(two[i])).astype(BF)
         slopes.append(silu_slope(two[i]))
     gather2.start()
-    for d in depths:
-        gather1.pump_xy(d)
-    first(fab.row_x)
-    first(fab.row_y)
+    gather1.pump_xy(0)
+    gather1.pump_xy(1)
+    gather2.land_z(1)
+    gather1.pump_xy(2)
+    gather2.land_z(2)
+    gather1.pump_xy(3)
     d_two = scatter1.finish()
     for i, part in enumerate(chunks):
         gt[fab.row + 1, :, part] = (d_two[:, part] * slopes[i]).astype(BF)
@@ -493,11 +550,14 @@
             gt_recv.at[fab.row],
             (r, fab.ch),
         )
+    gather2.land_z(3)
+    gather2.landed_z()
+    for d in depths[1:]:
+        gather2.spread_z(d)
     for d in depths:
         gather1.pump_d(d)
-    for d in depths[1:]:
-        gather2.land_z(d)
-        gather2.spread_z(d)
+    first(fab.row_x)
+    first(fab.row_y)
     first(fab.row_d)
     for r in other_rows:
         fab.arrived(gt.at[r + 1], gt_recv.at[r])
@@ -589,6 +649,27 @@
         weight_grad(b2, cots, gw_out, local.at[pl.ds(4, 2)], d)
     for copy in fab.sent:
         copy.wait_send()
+    for go, copy in fab.held:
+
+        @pl.when(go)
+        def _():
+            copy().wait_send()
+
+
+def hand_over(*refs):
+    count = len(refs) // 2
+    sems = refs[-1]
+    copies = []
+    for n, (src, dst) in enumerate(zip(refs[:count], refs[count : 2 * count])):
+        parts = 4 if src.shape[0] % 1024 == 0 else 1
+        size = src.shape[0] // parts
+        for p in range(parts):
+            rows = pl.ds(p * size, size)
+            copies.append(pltpu.make_async_copy(src.at[rows], dst.at[rows], sems.at[n, p]))
+    for copy in copies:
+        copy.start()
+    for copy in copies:
+        copy.wait()
 
 
 def body(features, w_in, w_group, w_out, cotangent):
@@ -603,7 +684,7 @@
     gw = w_group.shape[2]
     dma = pltpu.SemaphoreType.DMA
     vmem = pltpu.VMEM
-    gather_sems = [dma((lanes, rows)), dma((zs - 1,)), dma((6,)), dma((6,)), dma((rows * zs,))]
+    gather_sems = [dma((lanes, rows)), dma((zs + 1,)), dma((6,)), dma((6,)), dma((rows * zs,))]
     part = vmem((zs, pixels, width), BF)
     scatter = [part, part, part, part, vmem((pixels, width), F32)]
     scatter += [dma((zs,)), dma((zs,)), dma((zs - 1,)), dma((zs,))]
@@ -627,7 +708,7 @@
     in_any = pl.BlockSpec(memory_space=pl.ANY)
     flat = jax.ShapeDtypeStruct((pixels, width), BF)
     weight = jax.ShapeDtypeStruct((channels, width), BF)
-    out, g_in, gw_in, gw_group, gw_out = pl.pallas_call(
+    results = pl.pallas_call(
         block_kernel,
         out_shape=[flat, flat, weight, jax.ShapeDtypeStruct((9, gw, width), BF), weight],
         in_specs=[in_vmem, in_any, in_vmem, in_any, in_vmem],
@@ -643,6 +724,14 @@
         w_out,
         cotangent.reshape(pixels, width),
     )
+    out, g_in, gw_in, gw_group, gw_out = pl.pallas_call(
+        hand_over,
+        out_shape=[jax.ShapeDtypeStruct(v.shape, v.dtype) for v in results],
+        in_specs=[in_any] * 5,
+        out_specs=[in_any] * 5,
+        scratch_shapes=[dma((5, 4))],
+        compiler_params=pltpu.CompilerParams(vmem_limit_bytes=60 * 1024 * 1024),
+    )(*results)
     return (
         out.reshape(features.shape),
         g_in.reshape(features.shape),

time: 146 us -> 415 us (2.84)
  the two profiles are of different devices: /device:TPU:26 before, /device:TPU:1 now
where the time goes in v4:
time: 415 us; the launch traced here: 413 us
  Pallas kernels  413 us (100%)
    pallas_call x1, Pallas kernels, body(): pl.pallas_call(hand_over, out_shape=[jax.ShapeDtypeStruct(v.shape, v.dtyp...  289 us
    pallas_call x1, Pallas kernels, body(): pl.pallas_call(block_kernel, out_shape=[flat, flat, weight, jax.ShapeDtyp...  124 us

profile of v4, /device:TPU:1, one launch (start us, length us, event | category | flops | bytes accessed | tf_op | source)
XLA Modules:
  0.0 413.5 jit_solution(15568255770125155909)
XLA Ops:
  0.6 123.7 %shard_map.92 = (bf16[256,512]{1,0:T(8,128)(2,1)}, bf16[256,512]{1,0:T(8,128)(2,1)}, bf16[4096,512]{1,0:T(8,128)(2,1)}, bf16[9,64,512]{2,1,0:T(8,128)(2,1)}, bf16[4096,512]{1,0:T(8,128)(2,1)}) custom-call(bf16[256,512]{1,0:T(8,128)(2,1)} %bitcast.7, bf16[4096,512]{1,0:T(8,128)(2,1)} %refs_1_.1, bf16[9,64,512]{2,1,0:T(8,128)(2,1)} %bitcast.6, ...), custom_call_target="tpu_custom_call" | custom-call | tf_op jit(solution)/shard_map/pallas_call | solution.py:711
  124.3 289.1 %shard_map.93 = (bf16[256,512]{1,0:T(8,128)(2,1)}, bf16[256,512]{1,0:T(8,128)(2,1)}, bf16[4096,512]{1,0:T(8,128)(2,1)}, bf16[9,64,512]{2,1,0:T(8,128)(2,1)}, bf16[4096,512]{1,0:T(8,128)(2,1)}) custom-call(bf16[256,512]{1,0:T(8,128)(2,1)} %get-tuple-element.15.refs_0_, bf16[256,512]{1,0:T(8,128)(2,1)} %get-tuple-element.16.refs_1_, ...), custom_call_target="tpu_custom_call" | custom-call | tf_op jit(solution)/shard_map/pallas_call | solution.py:727

commit v5 on v4

--- a/solution.py
+++ b/solution.py
@@ -454,6 +454,23 @@
     depths = range(fab.zs)
     load_in.wait()
 
+    def activate(r):
+        value = pre[r]
+        act[r + 1] = (value * jax.nn.sigmoid(value)).astype(BF)
+
+    def first_xy(d):
+        for r in (fab.row_x, fab.row_y):
+            gather1.from_twin(d, r)
+
+        def add(i, carry):
+            r = fab.row_x + lax.rem(i, 2) * (fab.row_y - fab.row_x)
+            k = fab.z_at(d) * 2 + i // 2
+            lines = pl.ds(pl.multiple_of(k * width, width), width)
+            pre[r] += dot(b1[k, r], w_in[lines, :])
+            return carry
+
+        lax.fori_loop(0, 4, add, 0)
+
     def first(r):
         for d in depths:
             gather1.from_twin(d, r)
@@ -465,8 +482,7 @@
             return carry
 
         lax.fori_loop(0, count_k, add, 0)
-        value = pre[r]
-        act[r + 1] = (value * jax.nn.sigmoid(value)).astype(BF)
+        activate(r)
 
     for d in depths[1:]:
         gather1.land_z(d)
@@ -530,15 +546,20 @@
         two.append(total)
     slopes = []
     for i, part in enumerate(chunks):
-        b2[fab.ch, fab.row, :, part] = (two[i] * jax.nn.sigmoid(two[i])).astype(BF)
+        b2[fab.ch, fab.row, part, :] = (two[i] * jax.nn.sigmoid(two[i])).T.astype(BF)
         slopes.append(silu_slope(two[i]))
     gather2.start()
+    pre[fab.row_x] = jnp.zeros((pixels, width), F32)
+    pre[fab.row_y] = jnp.zeros((pixels, width), F32)
     gather1.pump_xy(0)
     gather1.pump_xy(1)
+    first_xy(0)
     gather2.land_z(1)
     gather1.pump_xy(2)
+    first_xy(1)
     gather2.land_z(2)
     gather1.pump_xy(3)
+    first_xy(2)
     d_two = scatter1.finish()
     for i, part in enumerate(chunks):
         gt[fab.row + 1, :, part] = (d_two[:, part] * slopes[i]).astype(BF)
@@ -550,14 +571,15 @@
             gt_recv.at[fab.row],
             (r, fab.ch),
         )
+    first_xy(3)
     gather2.land_z(3)
     gather2.landed_z()
     for d in depths[1:]:
         gather2.spread_z(d)
     for d in depths:
         gather1.pump_d(d)
-    first(fab.row_x)
-    first(fab.row_y)
+    activate(fab.row_x)
+    activate(fab.row_y)
     first(fab.row_d)
     for r in other_rows:
         fab.arrived(gt.at[r + 1], gt_recv.at[r])
@@ -585,13 +607,21 @@
 
     def last(k, carry):
         lines = pl.ds(pl.multiple_of(k * width, width), width)
-        pre[0] += dot(b2[k, fab.row], w_out[lines, :])
+        pre[0] += dot_tn(b2[k, fab.row], w_out[lines, :])
         return carry
 
     lax.fori_loop(0, count_k, last, 0)
     out[...] = pre[0].astype(BF)
 
-    def weight_grad(left, right, result, sems, d):
+    def product_in(k):
+        left = b1[k].reshape(rows * pixels, width)
+        return dot_tn(left, g1[...].reshape(rows * pixels, width))
+
+    def product_out(k):
+        left = jnp.concatenate([b2[k, r] for r in range(rows)], axis=1)
+        return dot(left, cots[...].reshape(rows * pixels, width))
+
+    def weight_grad(product, result, sems, d):
         def store(slot):
             k = fab.z_at(d) * 2 + slot
             return pltpu.make_async_copy(
@@ -601,9 +631,7 @@
             )
 
         def step(slot, carry):
-            lhs = left[fab.z_at(d) * 2 + slot].reshape(rows * pixels, width)
-            rhs = right[...].reshape(rows * pixels, width)
-            full = dot_tn(lhs, rhs).astype(BF)
+            full = product(fab.z_at(d) * 2 + slot).astype(BF)
             if d > 0:
                 store(slot).wait()
             stage[slot] = full
@@ -616,7 +644,7 @@
                 store(slot).wait()
 
     for d in depths:
-        weight_grad(b1, g1, gw_in, local.at[pl.ds(2, 2)], d)
+        weight_grad(product_in, gw_in, local.at[pl.ds(2, 2)], d)
         gather2.pump_xy(d)
 
     for b in range(3):
@@ -639,14 +667,14 @@
 
         lax.fori_loop(0, 3, tap_grad, 0)
 
-    g_in[...] = (cot[...].astype(F32) + scatter2.finish()).astype(BF)
     for r in other_rows:
         fab.arrived(cots.at[r], cot_recv.at[r])
     for d in depths:
         gather2.pump_d(d)
         for r in other_rows:
             gather2.from_twin(d, r)
-        weight_grad(b2, cots, gw_out, local.at[pl.ds(4, 2)], d)
+        weight_grad(product_out, gw_out, local.at[pl.ds(4, 2)], d)
+    g_in[...] = (cot[...].astype(F32) + scatter2.finish()).astype(BF)
     for copy in fab.sent:
         copy.wait_send()
     for go, copy in fab.held:
@@ -657,19 +685,23 @@
 
 
 def hand_over(*refs):
-    count = len(refs) // 2
-    sems = refs[-1]
-    copies = []
-    for n, (src, dst) in enumerate(zip(refs[:count], refs[count : 2 * count])):
+    sources, results, held = refs[:5], refs[5:10], refs[10:15]
+    load_sems, store_sems = refs[15:]
+    loads, stores = [], []
+    for n, (src, mid, dst) in enumerate(zip(sources, held, results)):
         parts = 4 if src.shape[0] % 1024 == 0 else 1
         size = src.shape[0] // parts
         for p in range(parts):
             rows = pl.ds(p * size, size)
-            copies.append(pltpu.make_async_copy(src.at[rows], dst.at[rows], sems.at[n, p]))
-    for copy in copies:
-        copy.start()
-    for copy in copies:
-        copy.wait()
+            loads.append(pltpu.make_async_copy(src.at[rows], mid.at[rows], load_sems.at[n, p]))
+            stores.append(pltpu.make_async_copy(mid.at[rows], dst.at[rows], store_sems.at[n, p]))
+    for load in loads:
+        load.start()
+    for load, store in zip(loads, stores):
+        load.wait()
+        store.start()
+    for store in stores:
+        store.wait()
 
 
 def body(features, w_in, w_group, w_out, cotangent):
@@ -690,7 +722,7 @@
     scatter += [dma((zs,)), dma((zs,)), dma((zs - 1,)), dma((zs,))]
     scratch = [
         vmem((lanes, rows, pixels, width), BF),
-        vmem((lanes, rows, pixels, width), BF),
+        vmem((lanes, rows, width, pixels), BF),
         vmem((channels, width), BF),
         vmem((channels, width), BF),
         vmem((rows, pixels, width), F32),
@@ -729,7 +761,7 @@
         out_shape=[jax.ShapeDtypeStruct(v.shape, v.dtype) for v in results],
         in_specs=[in_any] * 5,
         out_specs=[in_any] * 5,
-        scratch_shapes=[dma((5, 4))],
+        scratch_shapes=[vmem(v.shape, v.dtype) for v in results] + [dma((5, 4)), dma((5, 4))],
         compiler_params=pltpu.CompilerParams(vmem_limit_bytes=60 * 1024 * 1024),
     )(*results)
     return (

time: 415 us -> 132 us (0.32)
  Pallas kernels: 413 us -> 131 us
    pallas_call x1, Pallas kernels: 289 us -> 7.29 us  [body(): pl.pallas_call(hand_over, out_shape=[jax.ShapeDtypeStruct(v.shape, v.dtyp...]
where the time goes in v5:
time: 132 us; the launch traced here: 131 us
  Pallas kernels  131 us (99%)
    pallas_call x1, Pallas kernels, body(): pl.pallas_call(block_kernel, out_shape=[flat, flat, weight, jax.ShapeDtyp...  123 us
    pallas_call x1, Pallas kernels, body(): pl.pallas_call(hand_over, out_shape=[jax.ShapeDtypeStruct(v.shape, v.dtyp...  7.29 us

profile of v5, /device:TPU:1, one launch (start us, length us, event | category | flops | bytes accessed | tf_op | source)
XLA Modules:
  0.0 131.4 jit_solution(17113204240552832818)
XLA Ops:
  0.6 123.5 %shard_map.92 = (bf16[256,512]{1,0:T(8,128)(2,1)}, bf16[256,512]{1,0:T(8,128)(2,1)}, bf16[4096,512]{1,0:T(8,128)(2,1)}, bf16[9,64,512]{2,1,0:T(8,128)(2,1)}, bf16[4096,512]{1,0:T(8,128)(2,1)}) custom-call(bf16[256,512]{1,0:T(8,128)(2,1)} %bitcast.7, bf16[4096,512]{1,0:T(8,128)(2,1)} %refs_1_.1, bf16[9,64,512]{2,1,0:T(8,128)(2,1)} %bitcast.6, ...), custom_call_target="tpu_custom_call" | custom-call | tf_op jit(solution)/shard_map/pallas_call | solution.py:743
  124.1 7.3 %shard_map.93 = (bf16[256,512]{1,0:T(8,128)(2,1)}, bf16[256,512]{1,0:T(8,128)(2,1)}, bf16[4096,512]{1,0:T(8,128)(2,1)}, bf16[9,64,512]{2,1,0:T(8,128)(2,1)}, bf16[4096,512]{1,0:T(8,128)(2,1)}) custom-call(bf16[256,512]{1,0:T(8,128)(2,1)} %get-tuple-element.15.refs_0_, bf16[256,512]{1,0:T(8,128)(2,1)} %get-tuple-element.16.refs_1_, ...), custom_call_target="tpu_custom_call" | custom-call | tf_op jit(solution)/shard_map/pallas_call | solution.py:759

commit v6 on v5

--- a/solution.py
+++ b/solution.py
@@ -390,8 +390,10 @@
 
 
 def block_kernel(*refs):
-    (feat, w_in_hbm, wg, w_out_hbm, cot, out, g_in, gw_in, gw_group, gw_out) = refs[:10]
+    (feat, w_in_hbm, wg, w_out_hbm, cot, out, g_in, gw_in, gw_group, mids, cot_rows) = refs[:11]
+    refs = refs[1:]
     (b1, b2, w_in, w_out, pre, act, gt, g1, cots, shifted, wide, stage) = refs[10:22]
+    act_t = refs[57]
     (r1, z1, x1, y1, t1, r2, z2, x2, y2, t2) = refs[22:32]
     s1, s2 = refs[32:41], refs[41:50]
     cot_send, cot_recv, gt_send, gt_recv, halo_send, halo_recv, local = refs[50:57]
@@ -617,10 +619,6 @@
         left = b1[k].reshape(rows * pixels, width)
         return dot_tn(left, g1[...].reshape(rows * pixels, width))
 
-    def product_out(k):
-        left = jnp.concatenate([b2[k, r] for r in range(rows)], axis=1)
-        return dot(left, cots[...].reshape(rows * pixels, width))
-
     def weight_grad(product, result, sems, d):
         def store(slot):
             k = fab.z_at(d) * 2 + slot
@@ -647,6 +645,13 @@
         weight_grad(product_in, gw_in, local.at[pl.ds(2, 2)], d)
         gather2.pump_xy(d)
 
+    def turn(q, carry):
+        at = pl.ds(pl.multiple_of(q * pixels, pixels), pixels)
+        act_t[:, at] = act[q].astype(F32).T.astype(BF)
+        return carry
+
+    lax.fori_loop(0, rows + 2, turn, 0)
+
     for b in range(3):
 
         def move(q, carry):
@@ -659,8 +664,8 @@
 
         def tap_grad(a, carry):
             for part in chunks:
-                lhs = act[pl.ds(a, rows), :, part].reshape(rows * pixels, chunk)
-                full = dot_tn(lhs, shifted[:, :, part].reshape(rows * pixels, chunk))
+                span = pl.ds(pl.multiple_of(a * pixels, pixels), rows * pixels)
+                full = dot(act_t[part, span], shifted[:, :, part].reshape(rows * pixels, chunk))
                 full = jnp.where(same, full, 0.0).reshape(chunk // gw, gw, chunk)
                 gw_group[a * 3 + b, :, part] = jnp.sum(full, axis=0).astype(BF)
             return carry
@@ -669,12 +674,18 @@
 
     for r in other_rows:
         fab.arrived(cots.at[r], cot_recv.at[r])
+    stores = [pltpu.make_async_copy(cots, cot_rows, local.at[4])]
+    stores[0].start()
     for d in depths:
         gather2.pump_d(d)
         for r in other_rows:
             gather2.from_twin(d, r)
-        weight_grad(product_out, gw_out, local.at[pl.ds(4, 2)], d)
+        pair = pl.ds(fab.z_at(d) * 2, 2)
+        stores.append(pltpu.make_async_copy(b2.at[pair], mids.at[pair], local.at[5 + d]))
+        stores[-1].start()
     g_in[...] = (cot[...].astype(F32) + scatter2.finish()).astype(BF)
+    for store in stores:
+        store.wait()
     for copy in fab.sent:
         copy.wait_send()
     for go, copy in fab.held:
@@ -684,24 +695,54 @@
             copy().wait_send()
 
 
-def hand_over(*refs):
-    sources, results, held = refs[:5], refs[5:10], refs[10:15]
-    load_sems, store_sems = refs[15:]
-    loads, stores = [], []
-    for n, (src, mid, dst) in enumerate(zip(sources, held, results)):
-        parts = 4 if src.shape[0] % 1024 == 0 else 1
+def finish_kernel(*refs):
+    out, g_in, gw_in, gw_group, mids, cots = refs[:6]
+    results, gw_out = refs[6:10], refs[10]
+    held = refs[11:15]
+    mid, cot, product = refs[15:18]
+    load_sems, store_sems, mid_sems, product_sems = refs[18:]
+    count, rows, width, pixels = mids.shape
+    load_cot = pltpu.make_async_copy(cots, cot, mid_sems.at[count])
+    load_cot.start()
+
+    def load_mid(k):
+        return pltpu.make_async_copy(mids.at[k], mid.at[k], mid_sems.at[k])
+
+    def store(k):
+        lines = pl.ds(pl.multiple_of(k * width, width), width)
+        return pltpu.make_async_copy(product.at[k], gw_out.at[lines, :], product_sems.at[k])
+
+    for k in range(count):
+        load_mid(k).start()
+    copies = []
+    for n, (src, via, dst) in enumerate(zip((out, g_in, gw_group, gw_in), held, results)):
+        parts = 4 if n == 3 else 1
         size = src.shape[0] // parts
         for p in range(parts):
-            rows = pl.ds(p * size, size)
-            loads.append(pltpu.make_async_copy(src.at[rows], mid.at[rows], load_sems.at[n, p]))
-            stores.append(pltpu.make_async_copy(mid.at[rows], dst.at[rows], store_sems.at[n, p]))
-    for load in loads:
-        load.start()
-    for load, store in zip(loads, stores):
-        load.wait()
-        store.start()
-    for store in stores:
-        store.wait()
+            at = pl.ds(p * size, size)
+            load = pltpu.make_async_copy(src.at[at], via.at[at], load_sems.at[n, p])
+            copies.append((load, pltpu.make_async_copy(via.at[at], dst.at[at], store_sems.at[n, p])))
+            load.start()
+    load_cot.wait()
+    steps = 4
+    each = count // steps
+
+    def step(k, carry):
+        load_mid(k).wait()
+        left = jnp.concatenate([mid[k, r] for r in range(rows)], axis=1)
+        product[k] = dot(left, cot[...].reshape(rows * pixels, width)).astype(BF)
+        store(k).start()
+        return carry
+
+    for at in range(steps):
+        lax.fori_loop(at * each, (at + 1) * each, step, 0)
+        for load, onward in copies[2 * at : 2 * at + 2]:
+            load.wait()
+            onward.start()
+    for load, onward in copies:
+        onward.wait()
+    for k in range(count):
+        store(k).wait()
 
 
 def body(features, w_in, w_group, w_out, cotangent):
@@ -735,20 +776,25 @@
         vmem((2, width, width), BF),
     ]
     scratch += gather_sems * 2 + scatter * 2
-    scratch += [dma((3,)), dma((rows,)), dma((3,)), dma((rows,)), dma((2,)), dma((2,)), dma((6,))]
+    scratch += [dma((3,)), dma((rows,)), dma((3,)), dma((rows,)), dma((2,)), dma((2,)), dma((9,))]
+    scratch += [vmem((width, (rows + 2) * pixels), BF)]
     in_vmem = pl.BlockSpec(memory_space=pltpu.VMEM)
     in_any = pl.BlockSpec(memory_space=pl.ANY)
     flat = jax.ShapeDtypeStruct((pixels, width), BF)
     weight = jax.ShapeDtypeStruct((channels, width), BF)
-    results = pl.pallas_call(
+    taps = jax.ShapeDtypeStruct((9, gw, width), BF)
+    mids = jax.ShapeDtypeStruct((lanes, rows, width, pixels), BF)
+    cot_rows = jax.ShapeDtypeStruct((rows, pixels, width), BF)
+    params = pltpu.CompilerParams(
+        collective_id=0, has_side_effects=True, vmem_limit_bytes=60 * 1024 * 1024
+    )
+    out, g_in, gw_in, gw_group, mid_all, cot_all = pl.pallas_call(
         block_kernel,
-        out_shape=[flat, flat, weight, jax.ShapeDtypeStruct((9, gw, width), BF), weight],
+        out_shape=[flat, flat, weight, taps, mids, cot_rows],
         in_specs=[in_vmem, in_any, in_vmem, in_any, in_vmem],
-        out_specs=[in_vmem, in_vmem, in_any, in_vmem, in_any],
+        out_specs=[in_vmem, in_vmem, in_any, in_vmem, in_any, in_any],
         scratch_shapes=scratch,
-        compiler_params=pltpu.CompilerParams(
-            collective_id=0, has_side_effects=True, vmem_limit_bytes=60 * 1024 * 1024
-        ),
+        compiler_params=params,
     )(
         features.reshape(pixels, width),
         w_in,
@@ -756,14 +802,16 @@
         w_out,
         cotangent.reshape(pixels, width),
     )
-    out, g_in, gw_in, gw_group, gw_out = pl.pallas_call(
-        hand_over,
-        out_shape=[jax.ShapeDtypeStruct(v.shape, v.dtype) for v in results],
-        in_specs=[in_any] * 5,
+    out, g_in, gw_group, gw_in, gw_out = pl.pallas_call(
+        finish_kernel,
+        out_shape=[flat, flat, taps, weight, weight],
+        in_specs=[in_any] * 6,
         out_specs=[in_any] * 5,
-        scratch_shapes=[vmem(v.shape, v.dtype) for v in results] + [dma((5, 4)), dma((5, 4))],
+        scratch_shapes=[vmem(v.shape, BF) for v in (flat, flat, taps, weight, mids, cot_rows)]
+        + [vmem((lanes, width, width), BF)]
+        + [dma((4, 4)), dma((4, 4)), dma((lanes + 1,)), dma((lanes,))],
         compiler_params=pltpu.CompilerParams(vmem_limit_bytes=60 * 1024 * 1024),
-    )(*results)
+    )(out, g_in, gw_in, gw_group, mid_all, cot_all)
     return (
         out.reshape(features.shape),
         g_in.reshape(features.shape),

time: 132 us -> 130 us (0.985)
  Pallas kernels: 131 us -> 129 us
    pallas_call x2, Pallas kernels: 131 us -> 129 us  [the longest x1 120 us: body(): pl.pallas_call(block_kernel, out_shape=[flat, flat, weight, taps, mids, c...]
where the time goes in v6:
time: 130 us
  Pallas kernels  129 us (99%)
    pallas_call x1, Pallas kernels, body(): pl.pallas_call(block_kernel, out_shape=[flat, flat, weight, taps, mids, c...  120 us
    pallas_call x1, Pallas kernels, body(): pl.pallas_call(finish_kernel, out_shape=[flat, flat, taps, weight, weight...  8.81 us

profile of v6, /device:TPU:1, one launch (start us, length us, event | category | flops | bytes accessed | tf_op | source)
XLA Modules:
  0.0 129.8 jit_solution(4872544520439309987)
XLA Ops:
  0.6 120.3 %shard_map.92 = (bf16[256,512]{1,0:T(8,128)(2,1)}, bf16[256,512]{1,0:T(8,128)(2,1)}, bf16[4096,512]{1,0:T(8,128)(2,1)}, bf16[9,64,512]{2,1,0:T(8,128)(2,1)}, bf1...) custom-call(bf16[256,512]{1,0:T(8,128)(2,1)} %bitcast.7, bf16[4096,512]{1,0:T(8,128)(2,1)} %refs_1_.1, ...), custom_call_target="tpu_custom_call" | custom-call | tf_op jit(solution)/shard_map/pallas_call | solution.py:791
  121.0 8.8 %shard_map.93 = (bf16[256,512]{1,0:T(8,128)(2,1)}, bf16[256,512]{1,0:T(8,128)(2,1)}, bf16[9,64,512]{2,1,0:T(8,128)(2,1)}, bf16[4096,512]{1,0:T(8,128)(2,1)}, bf16[4096,512]{1,0:T(8,128)(2,1)}) custom-call(bf16[256,512]{1,0:T(8,128)(2,1)} %get-tuple-element.16.refs_0_, bf16[256,512]{1,0:T(8,128)(2,1)} %get-tuple-element.17.refs_1_, ...), custom_call_target="tpu_custom_call" | custom-call | tf_op jit(solution)/shard_map/pallas_call | solution.py:805

commit v7 on v6

--- a/solution.py
+++ b/solution.py
@@ -580,6 +580,7 @@
         gather2.spread_z(d)
     for d in depths:
         gather1.pump_d(d)
+    gather2.pump_xy(0)
     activate(fab.row_x)
     activate(fab.row_y)
     first(fab.row_d)
@@ -602,18 +603,7 @@
     lax.fori_loop(0, rows, back, 0)
     scatter2.start(g1[fab.row], w_in)
     scatter2.middle(g1[fab.row], w_in)
-
-    for d in depths:
-        gather2.from_twin(d, fab.row)
-    pre[0] = feat[...].astype(F32)
-
-    def last(k, carry):
-        lines = pl.ds(pl.multiple_of(k * width, width), width)
-        pre[0] += dot_tn(b2[k, fab.row], w_out[lines, :])
-        return carry
-
-    lax.fori_loop(0, count_k, last, 0)
-    out[...] = pre[0].astype(BF)
+    gather2.pump_xy(1)
 
     def product_in(k):
         left = b1[k].reshape(rows * pixels, width)
@@ -643,7 +633,20 @@
 
     for d in depths:
         weight_grad(product_in, gw_in, local.at[pl.ds(2, 2)], d)
-        gather2.pump_xy(d)
+        if d + 2 < fab.zs:
+            gather2.pump_xy(d + 2)
+
+    for d in depths:
+        gather2.from_twin(d, fab.row)
+    pre[0] = feat[...].astype(F32)
+
+    def last(k, carry):
+        lines = pl.ds(pl.multiple_of(k * width, width), width)
+        pre[0] += dot_tn(b2[k, fab.row], w_out[lines, :])
+        return carry
+
+    lax.fori_loop(0, count_k, last, 0)
+    out[...] = pre[0].astype(BF)
 
     def turn(q, carry):
         at = pl.ds(pl.multiple_of(q * pixels, pixels), pixels)

time: 130 us -> 135 us (1.038)
  Pallas kernels: 129 us -> 134 us
    pallas_call x1, Pallas kernels: 120 us -> 126 us  [body(): pl.pallas_call(block_kernel, out_shape=[flat, flat, weight, taps, mids, c...]
where the time goes in v7:
time: 135 us
  Pallas kernels  134 us (99%)
    pallas_call x1, Pallas kernels, body(): pl.pallas_call(block_kernel, out_shape=[flat, flat, weight, taps, mids, c...  126 us
    pallas_call x1, Pallas kernels, body(): pl.pallas_call(finish_kernel, out_shape=[flat, flat, taps, weight, weight...  8.81 us

profile of v7, /device:TPU:1, one launch (start us, length us, event | category | flops | bytes accessed | tf_op | source)
XLA Modules:
  0.0 135.1 jit_solution(852173853957703411)
XLA Ops:
  0.6 125.6 %shard_map.92 = (bf16[256,512]{1,0:T(8,128)(2,1)}, bf16[256,512]{1,0:T(8,128)(2,1)}, bf16[4096,512]{1,0:T(8,128)(2,1)}, bf16[9,64,512]{2,1,0:T(8,128)(2,1)}, bf1...) custom-call(bf16[256,512]{1,0:T(8,128)(2,1)} %bitcast.7, bf16[4096,512]{1,0:T(8,128)(2,1)} %refs_1_.1, ...), custom_call_target="tpu_custom_call" | custom-call | tf_op jit(solution)/shard_map/pallas_call | solution.py:794
  126.3 8.8 %shard_map.93 = (bf16[256,512]{1,0:T(8,128)(2,1)}, bf16[256,512]{1,0:T(8,128)(2,1)}, bf16[9,64,512]{2,1,0:T(8,128)(2,1)}, bf16[4096,512]{1,0:T(8,128)(2,1)}, bf16[4096,512]{1,0:T(8,128)(2,1)}) custom-call(bf16[256,512]{1,0:T(8,128)(2,1)} %get-tuple-element.16.refs_0_, bf16[256,512]{1,0:T(8,128)(2,1)} %get-tuple-element.17.refs_1_, ...), custom_call_target="tpu_custom_call" | custom-call | tf_op jit(solution)/shard_map/pallas_call | solution.py:808
